TPU v7x, 32 devices: a whole 2x2x4 slice. The times are simulated.
32 devices in a mesh: month: 4 (over y, core), cols: 8 (over z, x).
Axes of the slice: x: 2, y: 2, z: 4, core: 2. Of those that a mesh axis runs over, the one named last changes fastest.
Arguments:
- forcing: float32 [4, 128, 6, 128], P('month', 'cols'), may hold values from -6 to 6
- tiles: bfloat16 [4, 2048, 128, 128], P('month', 'cols'), may hold values from -0.21875 to 0.21875
- tile_rows: int32 [4, 2048], P('month', 'cols'), may hold values from 0 to 127, as said below
- tile_cols: int32 [4, 2048], P('month', 'cols'), may hold values from 0 to 127, as said below
- tile_count: int32 [4, 8], P('month', 'cols'), may hold values from 1 to 256, as said below
- depth: int32 [128, 16], P('cols'), may hold values from 1 to 8
Outputs:
- adjoint: float32 [4, 128, 6, 128], P('month', 'cols')
Inputs may be any that keep to these rules, and one draw needn't show every extreme that they name: `tile_cols`: the tiles held by cols index c take their column blocks from c's own blocks, c * 16 to (c + 1) * 16 - 1. `tile_rows`: the tiles held by cols index c take their row blocks from the blocks of c, of its two neighbours c - 1 and c + 1, and of the index c + 4, all counted modulo 128 / 16. `tile_count`: in each month one cols index has all 256 slots live; slots from the count on are unused.
All inputs are finite; a program needn't handle non-finite values.
Results may differ from a plain program's by a relative error of at most 0.022.
Values may be sent and summed in bfloat16 or wider, within the bound.
No kernel may reach another device: no remote copies, remote signals or barrier semaphores. Data moves between devices by JAX's collectives and lax.ppermute only.
A program may use at most 64 MiB of HBM per device.

v0:
```python
import jax
import jax.numpy as jnp
from jax import lax
from jax.sharding import PartitionSpec as P


def from_behind(shard, axis, by):
    length = lax.axis_size(axis)
    return lax.ppermute(shard, axis, [(i, (i + by) % length) for i in range(length)])


def wet_mask(depth, block):
    width = depth.shape[1]
    level = jnp.arange(block, dtype=jnp.int32) // width
    spread = jnp.tile(depth, (1, block // width))
    return (level[None, :] < spread).astype(jnp.float32)[:, None, :]


def place(buffer, terms, target, inside):
    return buffer.at[target].add(terms * inside.astype(jnp.float32)[:, None, None])


def terms_for(x_vals, active, plates, rows_all, local_cols, count, target_fn, span):
    slots = plates.shape[0]
    tracers = x_vals.shape[1]
    block = x_vals.shape[2]
    empty = jnp.zeros((span, tracers, block), jnp.float32)

    def compute(unused):
        picked = x_vals[local_cols]
        terms = jnp.einsum("stj,sij->sti", picked, plates, preferred_element_type=jnp.float32)
        valid = jnp.arange(slots, dtype=jnp.int32) < count
        target, inside = target_fn(rows_all)
        return place(empty, terms, target, inside & valid)

    return lax.cond(active, compute, lambda unused: empty, 0)


def on_device(forcing, tiles, tile_rows, tile_cols, tile_count, depth):
    months = lax.axis_size("month")
    my_month = lax.axis_index("month")
    ncols = lax.axis_size("cols")
    my_cols = lax.axis_index("cols")
    blk_local, tracers, block = forcing.shape[1:]
    nblk = blk_local * ncols
    wet = wet_mask(depth, block)

    def reduce_terms(x_vals, active, plates, rows_all, local_cols, count):

        def target_fn(rows):
            return (rows, rows >= 0)

        partial_terms = terms_for(
            x_vals, active, plates, rows_all, local_cols, count, target_fn, nblk
        )
        return lax.psum_scatter(
            partial_terms.astype(jnp.bfloat16), "cols", scatter_dimension=0, tiled=True
        ).astype(jnp.float32)

    def turn(step, carry):
        received, result = carry
        month_now = months - 1 - step % months
        active = my_month == month_now
        plates = tiles[0]
        rows_all = tile_rows[0]
        cols_here = tile_cols[0]
        count = tile_count[0, 0]
        own = forcing[0]
        local_cols = cols_here - my_cols * blk_local
        x_vals = (received + own).astype(jnp.bfloat16)
        summed = reduce_terms(x_vals, active, plates, rows_all, local_cols, count)
        state = wet * summed
        result = jnp.where((my_month == month_now) & (step >= months), state, result)
        sending = jnp.where(active, state, jnp.zeros_like(state))
        received = from_behind(sending.astype(jnp.bfloat16), "month", -1).astype(sending.dtype)
        return (received, result)

    start_state = jnp.zeros((blk_local, tracers, block), jnp.float32)
    final_carry, result = lax.fori_loop(0, 2 * months, turn, (start_state, start_state))
    return result[None]


def solution(mesh):
    in_specs = (
        P("month", "cols", None, None),
        P("month", "cols", None, None),
        P("month", "cols"),
        P("month", "cols"),
        P("month", "cols"),
        P("cols", None),
    )
    out_specs = P("month", "cols", None, None)
    return jax.shard_map(
        on_device, mesh=mesh, in_specs=in_specs, out_specs=out_specs, check_vma=False
    )
```

profile of v0, /device:TPU:0, one launch (start us, length us, event | category | flops | bytes accessed | tf_op | source)
XLA Modules:
  0.0 822.2 jit_solution(9649987843442033353)
XLA Ops:
  6.5 0.8 copy.9
  7.4 807.4 %while.18 = (s32[]{:T(128)}, f32[16,6,128]{2,1,0:T(8,128)S(1)}, f32[16,6,128]{2,1,0:T(8,128)S(1)}, s32[]{:T(128)}, f32[1,16,6,128]{3,2,1,0:T(8,128)S(1)}, /*inde...) while((s32[]{:T(128)}, f32[16,6,128]{2,1,0:T(8,128)S(1)}, ...), condition=%wide.region_5.6_spmd.clone, body=%wide.region_0.5_spmd.clone.sunk | while | flops 50953996 | bytes 14946738 | solution.py:79
  7.5 0.8 conditional.3
  7.5 0.8 broadcast.102
  8.3 1.8 convert_element_type.103
  10.2 98.5 %reduce-scatter.2.cloned.1.call-done = bf16[16,6,128]{2,1,0:T(8,128)(2,1)} async-done(((bf16[128,6,128]{2,1,0:T(8,128)(2,1)}), bf16[16,6,128]{2,1,0:T(8,128)(2,1)}) %reduce-scatter.2.cloned.1.call-update) | async-done | bytes 24592 | tf_op jit(solution)/shard_map/while/body/eval_jaxpr/reduce_scatter | solution.py:56
  109.6 1.6 collective-permute-done
  111.3 0.8 conditional.3
  111.3 0.8 broadcast.102
  112.1 1.8 convert_element_type.103
  114.0 95.3 %reduce-scatter.2.cloned.1.call-done = bf16[16,6,128]{2,1,0:T(8,128)(2,1)} async-done(((bf16[128,6,128]{2,1,0:T(8,128)(2,1)}), bf16[16,6,128]{2,1,0:T(8,128)(2,1)}) %reduce-scatter.2.cloned.1.call-update) | async-done | bytes 24592 | tf_op jit(solution)/shard_map/while/body/eval_jaxpr/reduce_scatter | solution.py:56
  210.1 1.6 collective-permute-done
  211.8 0.8 conditional.3
  211.8 0.8 broadcast.102
  212.7 1.8 convert_element_type.103
  214.6 95.6 %reduce-scatter.2.cloned.1.call-done = bf16[16,6,128]{2,1,0:T(8,128)(2,1)} async-done(((bf16[128,6,128]{2,1,0:T(8,128)(2,1)}), bf16[16,6,128]{2,1,0:T(8,128)(2,1)}) %reduce-scatter.2.cloned.1.call-update) | async-done | bytes 24592 | tf_op jit(solution)/shard_map/while/body/eval_jaxpr/reduce_scatter | solution.py:56
  311.1 1.6 collective-permute-done
  312.7 35.8 %conditional.3 = (f32[128,6,128]{2,1,0:T(8,128)}) conditional(s32[]{:T(128)} %convert_element_type.102, () %tuple.56, (s32[1,256]{1,0:T(1,128)}, s32[]{:T(128)}, s32[1,256]{1,0:T(1,128)}, bf16[16,6,128]{2,1,0:T(8,128)(2,1)S(1)}, bf16[1,256,128,128]{3,2,1,0:T(8,128)(2,1)}, /*index=5*/s32[1,1]{1,0:T(1,128)}) %tuple.57), branch_computations={%region_1.1_spmd, %region_2.3_spmd} | conditional | flops 50728704 | bytes 13122068 | solution.py:36
  313.5 0.8 gather_fusion
  315.7 6.7 fusion.4
  322.4 0.8 broadcast.103
  323.2 25.4 %scatter_fusion = f32[128,6,128]{2,1,0:T(8,128)} fusion(f32[128,6,128]{2,1,0:T(8,128)} %broadcast.103, s32[256]{0:T(256)S(1)} %bitcast.26, f32[256,6,128]{2,1,0:T(8,128)S(1)} %fusion.4), kind=kCustom, calls=%fused_computation.1 | custom fusion | flops 196608 | bytes 2360320 | tf_op jit(solution)/shard_map/while/body/eval_jaxpr/cond/branch_1_fun/scatter-add | solution.py:20
  348.6 1.8 convert_element_type.103
  350.5 59.5 %reduce-scatter.2.cloned.1.call-done = bf16[16,6,128]{2,1,0:T(8,128)(2,1)} async-done(((bf16[128,6,128]{2,1,0:T(8,128)(2,1)}), bf16[16,6,128]{2,1,0:T(8,128)(2,1)}) %reduce-scatter.2.cloned.1.call-update) | async-done | bytes 24592 | tf_op jit(solution)/shard_map/while/body/eval_jaxpr/reduce_scatter | solution.py:56
  410.8 1.6 collective-permute-done
  412.5 0.8 conditional.3
  412.5 0.8 broadcast.102
  413.4 1.8 convert_element_type.103
  415.3 95.7 %reduce-scatter.2.cloned.1.call-done = bf16[16,6,128]{2,1,0:T(8,128)(2,1)} async-done(((bf16[128,6,128]{2,1,0:T(8,128)(2,1)}), bf16[16,6,128]{2,1,0:T(8,128)(2,1)}) %reduce-scatter.2.cloned.1.call-update) | async-done | bytes 24592 | tf_op jit(solution)/shard_map/while/body/eval_jaxpr/reduce_scatter | solution.py:56
  511.8 1.6 collective-permute-done
  513.5 0.8 conditional.3
  513.5 0.8 broadcast.102
  514.3 1.8 convert_element_type.103
  516.2 95.4 %reduce-scatter.2.cloned.1.call-done = bf16[16,6,128]{2,1,0:T(8,128)(2,1)} async-done(((bf16[128,6,128]{2,1,0:T(8,128)(2,1)}), bf16[16,6,128]{2,1,0:T(8,128)(2,1)}) %reduce-scatter.2.cloned.1.call-update) | async-done | bytes 24592 | tf_op jit(solution)/shard_map/while/body/eval_jaxpr/reduce_scatter | solution.py:56
  612.4 1.6 collective-permute-done
  614.1 0.8 conditional.3
  614.1 0.8 broadcast.102
  614.9 1.8 convert_element_type.103
  616.8 95.7 %reduce-scatter.2.cloned.1.call-done = bf16[16,6,128]{2,1,0:T(8,128)(2,1)} async-done(((bf16[128,6,128]{2,1,0:T(8,128)(2,1)}), bf16[16,6,128]{2,1,0:T(8,128)(2,1)}) %reduce-scatter.2.cloned.1.call-update) | async-done | bytes 24592 | tf_op jit(solution)/shard_map/while/body/eval_jaxpr/reduce_scatter | solution.py:56
  713.4 1.6 collective-permute-done
  715.1 35.8 %conditional.3 = (f32[128,6,128]{2,1,0:T(8,128)}) conditional(s32[]{:T(128)} %convert_element_type.102, () %tuple.56, (s32[1,256]{1,0:T(1,128)}, s32[]{:T(128)}, s32[1,256]{1,0:T(1,128)}, bf16[16,6,128]{2,1,0:T(8,128)(2,1)S(1)}, bf16[1,256,128,128]{3,2,1,0:T(8,128)(2,1)}, /*index=5*/s32[1,1]{1,0:T(1,128)}) %tuple.57), branch_computations={%region_1.1_spmd, %region_2.3_spmd} | conditional | flops 50728704 | bytes 13122068 | solution.py:36
  715.8 0.8 gather_fusion
  718.0 6.7 fusion.4
  724.7 0.8 broadcast.103
  725.5 25.4 %scatter_fusion = f32[128,6,128]{2,1,0:T(8,128)} fusion(f32[128,6,128]{2,1,0:T(8,128)} %broadcast.103, s32[256]{0:T(256)S(1)} %bitcast.26, f32[256,6,128]{2,1,0:T(8,128)S(1)} %fusion.4), kind=kCustom, calls=%fused_computation.1 | custom fusion | flops 196608 | bytes 2360320 | tf_op jit(solution)/shard_map/while/body/eval_jaxpr/cond/branch_1_fun/scatter-add | solution.py:20
  750.9 1.8 convert_element_type.103
  752.8 59.5 %reduce-scatter.2.cloned.1.call-done = bf16[16,6,128]{2,1,0:T(8,128)(2,1)} async-done(((bf16[128,6,128]{2,1,0:T(8,128)(2,1)}), bf16[16,6,128]{2,1,0:T(8,128)(2,1)}) %reduce-scatter.2.cloned.1.call-update) | async-done | bytes 24592 | tf_op jit(solution)/shard_map/while/body/eval_jaxpr/reduce_scatter | solution.py:56
  813.2 1.6 collective-permute-done
  (100 shorter events, 12.9 us)
Async XLA Ops:
  7.4 2.7 copy-start
  7.4 101.3 %reduce-scatter.2.cloned.1.call-start = ((), (), s32[]{:S(2)}) async-start(), calls=%async_computation.1 | async-start | bytes 294912 | tf_op jit(solution)/shard_map/while/body/eval_jaxpr/reduce_scatter | solution.py:56
  109.5 1.7 collective-permute-start
  111.2 2.7 copy-start
  111.2 98.1 %reduce-scatter.2.cloned.1.call-start = ((), (), s32[]{:S(2)}) async-start(), calls=%async_computation.1 | async-start | bytes 294912 | tf_op jit(solution)/shard_map/while/body/eval_jaxpr/reduce_scatter | solution.py:56
  210.1 1.7 collective-permute-start
  211.7 2.7 copy-start
  211.7 98.5 %reduce-scatter.2.cloned.1.call-start = ((), (), s32[]{:S(2)}) async-start(), calls=%async_computation.1 | async-start | bytes 294912 | tf_op jit(solution)/shard_map/while/body/eval_jaxpr/reduce_scatter | solution.py:56
  311.0 1.7 collective-permute-start
  312.6 37.7 %copy-start = (s32[16,16]{1,0:T(8,128)S(1)}, s32[16,16]{1,0:T(8,128)}, u32[]{:S(2)}) copy-start(s32[16,16]{1,0:T(8,128)} %get-tuple-element.521) | copy-start | bytes 3076 | tf_op jit(solution)/shard_map/while
  312.7 97.3 %reduce-scatter.2.cloned.1.call-start = ((), (), s32[]{:S(2)}) async-start(), calls=%async_computation.1 | async-start | bytes 294912 | tf_op jit(solution)/shard_map/while/body/eval_jaxpr/reduce_scatter | solution.py:56
  410.8 1.7 collective-permute-start
  412.4 2.7 copy-start
  412.4 98.5 %reduce-scatter.2.cloned.1.call-start = ((), (), s32[]{:S(2)}) async-start(), calls=%async_computation.1 | async-start | bytes 294912 | tf_op jit(solution)/shard_map/while/body/eval_jaxpr/reduce_scatter | solution.py:56
  511.7 1.7 collective-permute-start
  513.4 2.7 copy-start
  513.4 98.2 %reduce-scatter.2.cloned.1.call-start = ((), (), s32[]{:S(2)}) async-start(), calls=%async_computation.1 | async-start | bytes 294912 | tf_op jit(solution)/shard_map/while/body/eval_jaxpr/reduce_scatter | solution.py:56
  612.4 1.7 collective-permute-start
  614.0 2.7 copy-start
  614.0 98.5 %reduce-scatter.2.cloned.1.call-start = ((), (), s32[]{:S(2)}) async-start(), calls=%async_computation.1 | async-start | bytes 294912 | tf_op jit(solution)/shard_map/while/body/eval_jaxpr/reduce_scatter | solution.py:56
  713.3 1.7 collective-permute-start
  715.0 37.7 %copy-start = (s32[16,16]{1,0:T(8,128)S(1)}, s32[16,16]{1,0:T(8,128)}, u32[]{:S(2)}) copy-start(s32[16,16]{1,0:T(8,128)} %get-tuple-element.521) | copy-start | bytes 3076 | tf_op jit(solution)/shard_map/while
  715.0 97.3 %reduce-scatter.2.cloned.1.call-start = ((), (), s32[]{:S(2)}) async-start(), calls=%async_computation.1 | async-start | bytes 294912 | tf_op jit(solution)/shard_map/while/body/eval_jaxpr/reduce_scatter | solution.py:56
  813.1 1.7 collective-permute-start
Sparse Core Ops, SparseCore 0:
  11.6 97.1 reduce-scatter.1
  115.4 93.8 reduce-scatter.1
  215.9 94.2 reduce-scatter.1
  350.5 59.4 reduce-scatter.1
  416.3 94.5 reduce-scatter.1
  517.2 94.2 reduce-scatter.1
  618.2 94.3 reduce-scatter.1
  752.8 59.4 reduce-scatter.1
where the time goes:
time: 826 us; the launch traced here: 822 us
  waiting for transfers between devices  708 us (86%)
  other arithmetic  75.4 us (9%)
  matrix products  13.4 us (2%)
  between operations  13.4 us (2%)
  local copies, waits for them, and re-layouts  10.4 us (1%)
    reduce_scatter x8, waiting for transfers between devices, reduce_terms(): lax.psum_scatter(partial_terms.astype(jnp.bfloat16), 'cols', scatter_dime...  695 us
    scatter-add x2, other arithmetic, place(): buffer.at[target].add(terms * inside.astype(jnp.float32)[:, None, None])  50.8 us
  transfers between devices with their start and end apart: 16, of which 16 were waited for; matrix products, arithmetic and copies ran while one was open for 0% of the time, Pallas kernels for 0%

commit v1 on v0

v1 whole, which is shorter than its diff:
```python
import functools

import jax
import jax.numpy as jnp
from jax import lax
from jax.experimental import pallas as pl
from jax.experimental.pallas import tpu as pltpu
from jax.sharding import PartitionSpec as P

SUB = 8
GROUP = 64
NT = (((1,), (1,)), ((), ()))


def wet_mask(depth, block):
    width = depth.shape[1]
    level = jnp.arange(block, dtype=jnp.int32) // width
    spread = jnp.tile(depth, (1, block // width))
    return (level[None, :] < spread).astype(jnp.float32)


def padded(values, rows):
    blocks, tracers, block = values.shape
    values = jnp.pad(values, ((0, 0), (0, rows - tracers), (0, 0)))
    return values.reshape(blocks * rows, block)


def products(live, slots, tiles, x, acc):
    acc[...] = jnp.zeros_like(acc)
    block = tiles.shape[-1]

    def round_of(g, carry):
        first = g * GROUP
        terms = []
        for u in range(0, GROUP, 2):
            s = first + u
            pair = jnp.concatenate([x[slots[1, s]], x[slots[1, s + 1]]], axis=0)
            both = tiles[pl.ds(s, 2)].reshape(2 * block, block)
            terms.append(
                lax.dot_general(pair.astype(jnp.bfloat16), both, NT, preferred_element_type=jnp.float32)
            )
        for u in range(0, GROUP, 2):
            s = first + u
            term = terms[u // 2]
            acc[slots[0, s]] += term[:SUB, :block]
            acc[slots[0, s + 1]] += term[SUB:, block:]
        return carry

    lax.fori_loop(0, (live + GROUP - 1) // GROUP, round_of, 0)


def step_kernel(first, live, slots, wet, forcing, tiles, *refs):
    refs = list(refs)
    arrived = [] if first else [refs.pop(0) for _ in range(4)]
    x, acc = refs[-2:]
    outs = refs[:4]
    own = x.shape[0]

    @pl.when(live[0] > 0)
    def _():
        if first:
            total = forcing[...]
        else:
            state = arrived[0][...].astype(jnp.float32)
            for ref in arrived[1:]:
                state += ref[...].astype(jnp.float32)
            state *= wet[...]
            refs[4][...] = state
            total = state + forcing[...]
        x[...] = total.reshape(x.shape)
        products(live[0], slots, tiles, x, acc)
        for d, out in enumerate(outs):
            out[...] = acc[pl.ds(d * own, own)].reshape(out.shape).astype(out.dtype)


def month_terms(live, slots, wet, forcing, tiles, arrived):
    rows, block = forcing.shape
    own = rows // SUB
    in_vmem = pl.BlockSpec(memory_space=pltpu.VMEM)
    in_smem = pl.BlockSpec(memory_space=pltpu.SMEM)
    first = arrived is None
    out_shape = [jax.ShapeDtypeStruct((rows, block), jnp.bfloat16)] * 4
    if not first:
        out_shape = out_shape + [jax.ShapeDtypeStruct((rows, block), jnp.float32)]
    operands = [live, slots, wet, forcing, tiles] + ([] if first else list(arrived))
    result = pl.pallas_call(
        functools.partial(step_kernel, first),
        out_shape=out_shape,
        in_specs=[in_smem] * 2 + [in_vmem] * (len(operands) - 2),
        out_specs=[in_vmem] * len(out_shape),
        scratch_shapes=[
            pltpu.VMEM((own, SUB, block), jnp.float32),
            pltpu.VMEM((4 * own + 1, SUB, block), jnp.float32),
        ],
        compiler_params=pltpu.CompilerParams(vmem_limit_bytes=16 * 2**20),
    )(*operands)
    return result[:4], (None if first else result[4])


def idle_chain(active, months):
    to = (active - 1) % months
    if months != 4:
        return [(to - k) % months for k in range(1, months - 1)]
    if active ^ 1 == to:
        return [to ^ 2, to ^ 3]
    return [to ^ 1, active ^ 1]


def hops(active, months, ncols, move):
    chain = [(active - 1) % months] + idle_chain(active, months) + [active]
    pairs = [(active * ncols + c, chain[0] * ncols + move(c) % ncols) for c in range(ncols)]
    for source, target in zip(chain, chain[1:]):
        pairs += [(source * ncols + c, target * ncols + c) for c in range(ncols)]
    return pairs


def on_device(forcing, tiles, tile_rows, tile_cols, tile_count, depth):
    months = lax.axis_size("month")
    my_month = lax.axis_index("month")
    ncols = lax.axis_size("cols")
    my_cols = lax.axis_index("cols")
    own, tracers, block = forcing.shape[1:]
    axes = ("month", "cols")
    moves = [lambda c: c - 1, lambda c: c + 1, lambda c: c + ncols // 2, lambda c: c]
    shifts = [ncols - 1, 1, ncols // 2, 0]

    count = tile_count[0, 0]
    owner = (tile_rows[0] // own - my_cols) % ncols
    place = sum(jnp.where(owner == shift, d * own, 0) for d, shift in enumerate(shifts))
    slot = jnp.arange(tile_rows.shape[1], dtype=jnp.int32)
    row = jnp.where(slot < count, place + tile_rows[0] % own, 4 * own)
    slots = jnp.stack([row, tile_cols[0] % own])

    wet = jnp.broadcast_to(wet_mask(depth, block)[:, None, :], (own, SUB, block))
    wet = wet.reshape(own * SUB, block)
    force = padded(forcing[0], SUB)
    plates = pltpu.with_memory_space_constraint(tiles[0], pltpu.VMEM)

    arrived = None
    states = []
    for step in range(2 * months):
        month = months - 1 - step % months
        live = jnp.where(my_month == month, count, 0).reshape(1)
        terms, state = month_terms(live, slots, wet, force, plates, arrived)
        states.append(state)
        if step < 2 * months - 1:
            arrived = [
                lax.ppermute(term, axes, hops(month, months, ncols, move))
                for term, move in zip(terms, moves)
            ]

    held = states[-1]
    for month in range(1, months - 1):
        held = jnp.where(my_month == month, states[2 * months - 1 - month], held)
    passed = lax.ppermute(held, "month", [(m, (m + 1) % months) for m in range(months)])
    state = terms[3].astype(jnp.float32)
    for term, move in zip(terms[:3], moves):
        pairs = [(c, move(c) % ncols) for c in range(ncols)]
        state += lax.ppermute(term, "cols", pairs).astype(jnp.float32)
    result = jnp.where(my_month == 0, wet * state, passed)
    return result.reshape(1, own, SUB, block)[:, :, :tracers]


def solution(mesh):
    in_specs = (
        P("month", "cols", None, None),
        P("month", "cols", None, None),
        P("month", "cols"),
        P("month", "cols"),
        P("month", "cols"),
        P("cols", None),
    )
    out_specs = P("month", "cols", None, None)
    return jax.shard_map(
        on_device, mesh=mesh, in_specs=in_specs, out_specs=out_specs, check_vma=False
    )
```

time: 826 us -> 95.7 us (0.12)
  waiting for transfers between devices: 708 us -> 23.2 us
  other arithmetic: 75.4 us -> 0.78 us
  starting transfers between devices: 0.79 us -> 36.1 us
  matrix products: 13.4 us -> 0 us
  between operations: 13.4 us -> 0.8 us
  Pallas kernels: 0 us -> 12.5 us
  local copies, waits for them, and re-layouts: 10.4 us -> 22.5 us
    reduce_scatter x8 -> x0, waiting for transfers between devices: 695 us -> none  [reduce_terms(): lax.psum_scatter(partial_terms.astype(jnp.bfloat16), 'cols', scatter_dime...]
    scatter-add x2 -> x0, other arithmetic: 50.8 us -> none  [place(): buffer.at[target].add(terms * inside.astype(jnp.float32)[:, None, None])]
    ppermute x8 -> x32, starting transfers between devices: 0.46 us -> 36.1 us  [the longest x28 33.9 us: on_device(): lax.ppermute(term, axes, hops(month, months, ncols, move))]
    unnamed x1 -> x14, local copies, waits for them, and re-layouts: 0.82 us -> 21.7 us
    convert_element_type x26 -> x1, other arithmetic: 15.5 us -> 0.01 us  [wet_mask(): return (level[None, :] < spread).astype(jnp.float32)]
    dot_general x2 -> x0, matrix products: 13.4 us -> none  [compute(): jnp.einsum('stj,sij->sti', picked, plates, preferred_element_type=jnp.flo...]
    pallas_call x0 -> x8, Pallas kernels: none -> 12.5 us  [month_terms(): pl.pallas_call(functools.partial(step_kernel, first), out_shape=out_shape...]
    ppermute x8 -> x32, waiting for transfers between devices: 12.7 us -> 23.2 us  [the longest x28 17.6 us: on_device(): lax.ppermute(term, axes, hops(month, months, ncols, move))]
  transfers between devices with their start and end apart: 16 -> 32, of which waited for: 16 -> 20; matrix products, arithmetic and copies ran while one was open for 0% -> 0% of each run, Pallas kernels for 0% -> 0%
where the time goes in v1:
time: 95.7 us; the launch traced here: 95.9 us
  starting transfers between devices  36.1 us (38%)
  waiting for transfers between devices  23.2 us (24%)
  local copies, waits for them, and re-layouts  22.5 us (24%)
  Pallas kernels  12.5 us (13%)
    ppermute x28, starting transfers between devices, on_device(): lax.ppermute(term, axes, hops(month, months, ncols, move))  33.9 us
    unnamed x14, local copies, waits for them, and re-layouts  21.7 us
    ppermute x28, waiting for transfers between devices, on_device(): lax.ppermute(term, axes, hops(month, months, ncols, move))  17.6 us
    pallas_call x8, Pallas kernels, month_terms(): pl.pallas_call(functools.partial(step_kernel, first), out_shape=out_shape...  12.5 us
    ppermute x3, waiting for transfers between devices, on_device(): state += lax.ppermute(term, 'cols', pairs).astype(jnp.float32)  5.59 us
    ppermute x3, starting transfers between devices, on_device(): state += lax.ppermute(term, 'cols', pairs).astype(jnp.float32)  2.08 us
  transfers between devices with their start and end apart: 32, of which 20 were waited for; matrix products, arithmetic and copies ran while one was open for 0% of the time, Pallas kernels for 0%

profile of v1, /device:TPU:0, one launch (start us, length us, event | category | flops | bytes accessed | tf_op | source)
XLA Modules:
  0.0 95.9 jit_solution(14890427145485703882)
XLA Ops:
  0.7 0.8 copy.10
  1.5 0.7 tile.4
  2.3 0.7 and_select_fusion
  3.1 3.4 %copy-done = bf16[1,256,128,128]{3,2,1,0:T(8,128)(2,1)S(1)} copy-done((bf16[1,256,128,128]{3,2,1,0:T(8,128)(2,1)S(1)}, bf16[1,256,128,128]{3,2,1,0:T(8,128)(2,1)}, u32[]{:S(2)}) %copy-start) | copy-done | bytes 8388632
  6.4 0.6 shard_map.64
  7.0 0.5 collective-permute-start
  7.5 3.5 %collective-permute-start.1 = (bf16[128,128]{1,0:T(8,128)(2,1)S(1)}, bf16[128,128]{1,0:T(8,128)(2,1)S(1)}, u32[]{:S(2)}, u32[]{:S(2)}) collective-permute-start(bf16[128,128]{1,0:T(8,128)(2,1)S(1)} %get-tuple-element.41), channel_id=1, source_target_pairs={{24,17},{25,18},{26,19},{27,20},{28,21},{29,22},{30,23},{31,16},{1... | collective-permute-start | bytes 98312 | tf_op jit(solution)/shard_map/ppermute | solution.py:148
  11.0 3.4 %collective-permute-start.2 = (bf16[128,128]{1,0:T(8,128)(2,1)S(1)}, bf16[128,128]{1,0:T(8,128)(2,1)S(1)}, u32[]{:S(2)}, u32[]{:S(2)}) collective-permute-start(bf16[128,128]{1,0:T(8,128)(2,1)S(1)} %get-tuple-element.42), channel_id=1, source_target_pairs={{24,20},{25,21},{26,22},{27,23},{28,16},{29,17},{30,18},{31,19},{1... | collective-permute-start | bytes 98312 | tf_op jit(solution)/shard_map/ppermute | solution.py:148
  14.4 0.8 collective-permute-done.2.refs_2_
  15.3 3.1 %collective-permute-done.3.refs_3_ = bf16[128,128]{1,0:T(8,128)(2,1)S(1)} collective-permute-done((bf16[128,128]{1,0:T(8,128)(2,1)S(1)}, bf16[128,128]{1,0:T(8,128)(2,1)S(1)}, u32[]{:S(2)}, u32[]{:S(2)}) %collective-permute-start.3) | collective-permute-done | bytes 32800 | tf_op jit(solution)/shard_map/ppermute | solution.py:148
  18.3 3.4 %copy-done.1 = bf16[1,256,128,128]{3,2,1,0:T(8,128)(2,1)S(1)} copy-done((bf16[1,256,128,128]{3,2,1,0:T(8,128)(2,1)S(1)}, bf16[1,256,128,128]{3,2,1,0:T(8,128)(2,1)}, u32[]{:S(2)}) %copy-start.1) | copy-done | bytes 8388632
  21.7 1.2 %shard_map.65 = (bf16[128,128]{1,0:T(8,128)(2,1)S(1)}, bf16[128,128]{1,0:T(8,128)(2,1)S(1)}, bf16[128,128]{1,0:T(8,128)(2,1)S(1)}, bf16[128,128]{1,0:T(8,128)(2,1)S(1)}, f32[128,128]{1,0:T(8,128)}) custom-call(s32[1]{0:T(128)} %bitcast.7.live, s32[2,256]{1,0:T(2,128)S(1)} %pad_add_fusion.slots, f32[128,128]{1,0:T(8,128)S(1)} %get-tuple-element.78.wet, ...), custom_call_target="tpu_custom_call" | custom-call | tf_op jit(solution)/shard_map/pallas_call | solution.py:86
  22.9 0.5 collective-permute-start.5
  23.5 1.0 %collective-permute-done.4.refs_0_ = bf16[128,128]{1,0:T(8,128)(2,1)S(1)} collective-permute-done((bf16[128,128]{1,0:T(8,128)(2,1)S(1)}, bf16[128,128]{1,0:T(8,128)(2,1)S(1)}, u32[]{:S(2)}, u32[]{:S(2)}) %collective-permute-start.4) | collective-permute-done | bytes 32800 | tf_op jit(solution)/shard_map/ppermute | solution.py:148
  24.5 0.5 collective-permute-done.5.refs_1_
  25.7 3.4 %copy-done.2 = bf16[1,256,128,128]{3,2,1,0:T(8,128)(2,1)S(1)} copy-done((bf16[1,256,128,128]{3,2,1,0:T(8,128)(2,1)S(1)}, bf16[1,256,128,128]{3,2,1,0:T(8,128)(2,1)}, u32[]{:S(2)}) %copy-start.2) | copy-done | bytes 8388632
  29.0 1.2 %shard_map.66 = (bf16[128,128]{1,0:T(8,128)(2,1)S(1)}, bf16[128,128]{1,0:T(8,128)(2,1)S(1)}, bf16[128,128]{1,0:T(8,128)(2,1)S(1)}, bf16[128,128]{1,0:T(8,128)(2,1)S(1)}, f32[128,128]{1,0:T(8,128)}) custom-call(s32[1]{0:T(128)} %bitcast.6.live, s32[2,256]{1,0:T(2,128)S(1)} %pad_add_fusion.slots, f32[128,128]{1,0:T(8,128)S(1)} %get-tuple-element.78.wet, ...), custom_call_target="tpu_custom_call" | custom-call | tf_op jit(solution)/shard_map/pallas_call | solution.py:86
  30.2 1.5 %collective-permute-start.8 = (bf16[128,128]{1,0:T(8,128)(2,1)S(1)}, bf16[128,128]{1,0:T(8,128)(2,1)S(1)}, u32[]{:S(2)}, u32[]{:S(2)}) collective-permute-start(bf16[128,128]{1,0:T(8,128)(2,1)S(1)} %get-tuple-element.48), channel_id=1, source_target_pairs={{8,7},{9,0},{10,1},{11,2},{12,3},{13,4},{14,5},{15,6},{0,16},{1,17... | collective-permute-start | bytes 98312 | tf_op jit(solution)/shard_map/ppermute | solution.py:148
  31.8 0.7 collective-permute-start.9
  32.5 6.9 %collective-permute-start.10 = (bf16[128,128]{1,0:T(8,128)(2,1)S(1)}, bf16[128,128]{1,0:T(8,128)(2,1)S(1)}, u32[]{:S(2)}, u32[]{:S(2)}) collective-permute-start(bf16[128,128]{1,0:T(8,128)(2,1)S(1)} %get-tuple-element.50), channel_id=1, source_target_pairs={{8,4},{9,5},{10,6},{11,7},{12,0},{13,1},{14,2},{15,3},{0,16},{1,17... | collective-permute-start | bytes 98312 | tf_op jit(solution)/shard_map/ppermute | solution.py:148
  39.4 1.5 %collective-permute-done.10.refs_2_ = bf16[128,128]{1,0:T(8,128)(2,1)S(1)} collective-permute-done((bf16[128,128]{1,0:T(8,128)(2,1)S(1)}, bf16[128,128]{1,0:T(8,128)(2,1)S(1)}, u32[]{:S(2)}, u32[]{:S(2)}) %collective-permute-start.10) | collective-permute-done | bytes 32800 | tf_op jit(solution)/shard_map/ppermute | solution.py:148
  41.3 3.4 %copy-done.3 = bf16[1,256,128,128]{3,2,1,0:T(8,128)(2,1)S(1)} copy-done((bf16[1,256,128,128]{3,2,1,0:T(8,128)(2,1)S(1)}, bf16[1,256,128,128]{3,2,1,0:T(8,128)(2,1)}, u32[]{:S(2)}) %copy-start.3) | copy-done | bytes 8388632
  44.7 3.9 %shard_map.67 = (bf16[128,128]{1,0:T(8,128)(2,1)S(1)}, bf16[128,128]{1,0:T(8,128)(2,1)S(1)}, bf16[128,128]{1,0:T(8,128)(2,1)S(1)}, bf16[128,128]{1,0:T(8,128)(2,1)S(1)}, f32[128,128]{1,0:T(8,128)}) custom-call(s32[1]{0:T(128)} %bitcast.2.live, s32[2,256]{1,0:T(2,128)S(1)} %pad_add_fusion.slots, f32[128,128]{1,0:T(8,128)S(1)} %get-tuple-element.78.wet, ...), custom_call_target="tpu_custom_call" | custom-call | tf_op jit(solution)/shard_map/pallas_call | solution.py:86
  48.6 2.2 %collective-permute-start.15 = (bf16[128,128]{1,0:T(8,128)(2,1)S(1)}, bf16[128,128]{1,0:T(8,128)(2,1)S(1)}, u32[]{:S(2)}, u32[]{:S(2)}) collective-permute-start(bf16[128,128]{1,0:T(8,128)(2,1)S(1)} %get-tuple-element.55), channel_id=1, source_target_pairs={{0,24},{1,25},{2,26},{3,27},{4,28},{5,29},{6,30},{7,31},{24,16},{2... | collective-permute-start | bytes 98312 | tf_op jit(solution)/shard_map/ppermute | solution.py:148
  50.9 1.6 %collective-permute-done.15.refs_3_ = bf16[128,128]{1,0:T(8,128)(2,1)S(1)} collective-permute-done((bf16[128,128]{1,0:T(8,128)(2,1)S(1)}, bf16[128,128]{1,0:T(8,128)(2,1)S(1)}, u32[]{:S(2)}, u32[]{:S(2)}) %collective-permute-start.15) | collective-permute-done | bytes 32800 | tf_op jit(solution)/shard_map/ppermute | solution.py:148
  52.5 3.4 %copy-done.4 = bf16[1,256,128,128]{3,2,1,0:T(8,128)(2,1)S(1)} copy-done((bf16[1,256,128,128]{3,2,1,0:T(8,128)(2,1)S(1)}, bf16[1,256,128,128]{3,2,1,0:T(8,128)(2,1)}, u32[]{:S(2)}) %copy-start.4) | copy-done | bytes 8388632
  55.8 1.2 %shard_map.68 = (bf16[128,128]{1,0:T(8,128)(2,1)S(1)}, bf16[128,128]{1,0:T(8,128)(2,1)S(1)}, bf16[128,128]{1,0:T(8,128)(2,1)S(1)}, bf16[128,128]{1,0:T(8,128)(2,1)S(1)}, f32[128,128]{1,0:T(8,128)}) custom-call(s32[1]{0:T(128)} %bitcast.8.live, s32[2,256]{1,0:T(2,128)S(1)} %pad_add_fusion.slots, f32[128,128]{1,0:T(8,128)S(1)} %get-tuple-element.78.wet, ...), custom_call_target="tpu_custom_call" | custom-call | tf_op jit(solution)/shard_map/pallas_call | solution.py:86
  57.0 0.7 collective-permute-start.16
  57.7 3.7 %collective-permute-start.17 = (bf16[128,128]{1,0:T(8,128)(2,1)S(1)}, bf16[128,128]{1,0:T(8,128)(2,1)S(1)}, u32[]{:S(2)}, u32[]{:S(2)}) collective-permute-start(bf16[128,128]{1,0:T(8,128)(2,1)S(1)} %get-tuple-element.57), channel_id=1, source_target_pairs={{24,17},{25,18},{26,19},{27,20},{28,21},{29,22},{30,23},{31,16},{1... | collective-permute-start | bytes 98312 | tf_op jit(solution)/shard_map/ppermute | solution.py:148
  61.5 0.8 collective-permute-done.17.refs_1_
  62.3 3.1 %collective-permute-done.18.refs_2_ = bf16[128,128]{1,0:T(8,128)(2,1)S(1)} collective-permute-done((bf16[128,128]{1,0:T(8,128)(2,1)S(1)}, bf16[128,128]{1,0:T(8,128)(2,1)S(1)}, u32[]{:S(2)}, u32[]{:S(2)}) %collective-permute-start.18) | collective-permute-done | bytes 32800 | tf_op jit(solution)/shard_map/ppermute | solution.py:148
  65.3 0.4 collective-permute-done.19.refs_3_
  65.7 3.4 %copy-done.5 = bf16[1,256,128,128]{3,2,1,0:T(8,128)(2,1)S(1)} copy-done((bf16[1,256,128,128]{3,2,1,0:T(8,128)(2,1)S(1)}, bf16[1,256,128,128]{3,2,1,0:T(8,128)(2,1)}, u32[]{:S(2)}) %copy-start.5) | copy-done | bytes 8388632
  69.1 0.6 shard_map.69
  69.7 0.5 collective-permute-start.21
  70.3 1.0 %collective-permute-done.20.refs_0_ = bf16[128,128]{1,0:T(8,128)(2,1)S(1)} collective-permute-done((bf16[128,128]{1,0:T(8,128)(2,1)S(1)}, bf16[128,128]{1,0:T(8,128)(2,1)S(1)}, u32[]{:S(2)}, u32[]{:S(2)}) %collective-permute-start.20) | collective-permute-done | bytes 32800 | tf_op jit(solution)/shard_map/ppermute | solution.py:148
  71.3 0.5 collective-permute-done.21.refs_1_
  72.4 0.6 shard_map.70
  73.0 1.6 %collective-permute-start.24 = (bf16[128,128]{1,0:T(8,128)(2,1)S(1)}, bf16[128,128]{1,0:T(8,128)(2,1)S(1)}, u32[]{:S(2)}, u32[]{:S(2)}) collective-permute-start(bf16[128,128]{1,0:T(8,128)(2,1)S(1)} %get-tuple-element.64), channel_id=1, source_target_pairs={{8,7},{9,0},{10,1},{11,2},{12,3},{13,4},{14,5},{15,6},{0,16},{1,17... | collective-permute-start | bytes 98312 | tf_op jit(solution)/shard_map/ppermute | solution.py:148
  74.6 0.7 collective-permute-start.25
  75.3 7.0 %collective-permute-start.26 = (bf16[128,128]{1,0:T(8,128)(2,1)S(1)}, bf16[128,128]{1,0:T(8,128)(2,1)S(1)}, u32[]{:S(2)}, u32[]{:S(2)}) collective-permute-start(bf16[128,128]{1,0:T(8,128)(2,1)S(1)} %get-tuple-element.66), channel_id=1, source_target_pairs={{8,4},{9,5},{10,6},{11,7},{12,0},{13,1},{14,2},{15,3},{0,16},{1,17... | collective-permute-start | bytes 98312 | tf_op jit(solution)/shard_map/ppermute | solution.py:148
  82.3 1.5 %collective-permute-done.26.refs_2_ = bf16[128,128]{1,0:T(8,128)(2,1)S(1)} collective-permute-done((bf16[128,128]{1,0:T(8,128)(2,1)S(1)}, bf16[128,128]{1,0:T(8,128)(2,1)S(1)}, u32[]{:S(2)}, u32[]{:S(2)}) %collective-permute-start.26) | collective-permute-done | bytes 32800 | tf_op jit(solution)/shard_map/ppermute | solution.py:148
  84.2 3.3 %shard_map.71 = (bf16[128,128]{1,0:T(8,128)(2,1)S(1)}, bf16[128,128]{1,0:T(8,128)(2,1)S(1)}, bf16[128,128]{1,0:T(8,128)(2,1)S(1)}, bf16[128,128]{1,0:T(8,128)(2,1)S(1)}, f32[128,128]{1,0:T(8,128)S(1)}) custom-call(s32[1]{0:T(128)} %bitcast.2.live, s32[2,256]{1,0:T(2,128)S(1)} %pad_add_fusion.slots, f32[128,128]{1,0:T(8,128)S(1)} %get-tuple-element.78.wet, ...), custom_call_target="tpu_custom_call" | custom-call | tf_op jit(solution)/shard_map/pallas_call | solution.py:86
  87.6 1.1 %collective-permute-start.28 = (bf16[128,128]{1,0:T(8,128)(2,1)S(1)}, bf16[128,128]{1,0:T(8,128)(2,1)S(1)}, u32[]{:S(2)}, u32[]{:S(2)}) collective-permute-start(bf16[128,128]{1,0:T(8,128)(2,1)S(1)} %get-tuple-element.69), channel_id=1, source_target_pairs={{0,7},{1,0},{2,1},{3,2},{4,3},{5,4},{6,5},{7,6},{8,15},{9,8},{10,9... | collective-permute-start | bytes 98312 | tf_op jit(solution)/shard_map/ppermute | solution.py:159
  88.6 1.0 %collective-permute-start.29 = (bf16[128,128]{1,0:T(8,128)(2,1)S(1)}, bf16[128,128]{1,0:T(8,128)(2,1)S(1)}, u32[]{:S(2)}, u32[]{:S(2)}) collective-permute-start(bf16[128,128]{1,0:T(8,128)(2,1)S(1)} %get-tuple-element.70), channel_id=1, source_target_pairs={{0,1},{1,2},{2,3},{3,4},{4,5},{5,6},{6,7},{7,0},{8,9},{9,10},{10,1... | collective-permute-start | bytes 98312 | tf_op jit(solution)/shard_map/ppermute | solution.py:159
  89.6 1.9 %collective-permute-done.28 = bf16[128,128]{1,0:T(8,128)(2,1)S(1)} collective-permute-done((bf16[128,128]{1,0:T(8,128)(2,1)S(1)}, bf16[128,128]{1,0:T(8,128)(2,1)S(1)}, u32[]{:S(2)}, u32[]{:S(2)}) %collective-permute-start.28) | collective-permute-done | bytes 32800 | tf_op jit(solution)/shard_map/ppermute | solution.py:159
  91.5 3.7 %collective-permute-done.29 = bf16[128,128]{1,0:T(8,128)(2,1)S(1)} collective-permute-done((bf16[128,128]{1,0:T(8,128)(2,1)S(1)}, bf16[128,128]{1,0:T(8,128)(2,1)S(1)}, u32[]{:S(2)}, u32[]{:S(2)}) %collective-permute-start.29) | collective-permute-done | bytes 32800 | tf_op jit(solution)/shard_map/ppermute | solution.py:159
  95.3 0.6 copy.9
  (47 shorter events, 2.6 us)
Async XLA Ops:
  3.0 3.4 %copy-start = (bf16[1,256,128,128]{3,2,1,0:T(8,128)(2,1)S(1)}, bf16[1,256,128,128]{3,2,1,0:T(8,128)(2,1)}, u32[]{:S(2)}) copy-start(bf16[1,256,128,128]{3,2,1,0:T(8,128)(2,1)} %param.7) | copy-start | bytes 25165828
  7.0 7.4 %collective-permute-start = (bf16[128,128]{1,0:T(8,128)(2,1)S(1)}, bf16[128,128]{1,0:T(8,128)(2,1)S(1)}, u32[]{:S(2)}, u32[]{:S(2)}) collective-permute-start(bf16[128,128]{1,0:T(8,128)(2,1)S(1)} %get-tuple-element.40), channel_id=1, source_target_pairs={{24,23},{25,16},{26,17},{27,18},{28,19},{29,20},{30,21},{31,22},{1... | collective-permute-start | bytes 98312 | tf_op jit(solution)/shard_map/ppermute | solution.py:148
  7.5 6.9 %collective-permute-start.1 = (bf16[128,128]{1,0:T(8,128)(2,1)S(1)}, bf16[128,128]{1,0:T(8,128)(2,1)S(1)}, u32[]{:S(2)}, u32[]{:S(2)}) collective-permute-start(bf16[128,128]{1,0:T(8,128)(2,1)S(1)} %get-tuple-element.41), channel_id=1, source_target_pairs={{24,17},{25,18},{26,19},{27,20},{28,21},{29,22},{30,23},{31,16},{1... | collective-permute-start | bytes 98312 | tf_op jit(solution)/shard_map/ppermute | solution.py:148
  11.0 4.2 %collective-permute-start.2 = (bf16[128,128]{1,0:T(8,128)(2,1)S(1)}, bf16[128,128]{1,0:T(8,128)(2,1)S(1)}, u32[]{:S(2)}, u32[]{:S(2)}) collective-permute-start(bf16[128,128]{1,0:T(8,128)(2,1)S(1)} %get-tuple-element.42), channel_id=1, source_target_pairs={{24,20},{25,21},{26,22},{27,23},{28,16},{29,17},{30,18},{31,19},{1... | collective-permute-start | bytes 98312 | tf_op jit(solution)/shard_map/ppermute | solution.py:148
  14.4 3.9 %collective-permute-start.3 = (bf16[128,128]{1,0:T(8,128)(2,1)S(1)}, bf16[128,128]{1,0:T(8,128)(2,1)S(1)}, u32[]{:S(2)}, u32[]{:S(2)}) collective-permute-start(bf16[128,128]{1,0:T(8,128)(2,1)S(1)} %get-tuple-element.43), channel_id=1, source_target_pairs={{24,16},{25,17},{26,18},{27,19},{28,20},{29,21},{30,22},{31,23},{1... | collective-permute-start | bytes 98312 | tf_op jit(solution)/shard_map/ppermute | solution.py:148
  18.3 3.4 %copy-start.1 = (bf16[1,256,128,128]{3,2,1,0:T(8,128)(2,1)S(1)}, bf16[1,256,128,128]{3,2,1,0:T(8,128)(2,1)}, u32[]{:S(2)}) copy-start(bf16[1,256,128,128]{3,2,1,0:T(8,128)(2,1)} %param.7) | copy-start | bytes 25165828
  22.9 1.6 %collective-permute-start.4 = (bf16[128,128]{1,0:T(8,128)(2,1)S(1)}, bf16[128,128]{1,0:T(8,128)(2,1)S(1)}, u32[]{:S(2)}, u32[]{:S(2)}) collective-permute-start(bf16[128,128]{1,0:T(8,128)(2,1)S(1)} %get-tuple-element.44), channel_id=1, source_target_pairs={{16,15},{17,8},{18,9},{19,10},{20,11},{21,12},{22,13},{23,14},{8,0... | collective-permute-start | bytes 98312 | tf_op jit(solution)/shard_map/ppermute | solution.py:148
  22.9 2.1 %collective-permute-start.5 = (bf16[128,128]{1,0:T(8,128)(2,1)S(1)}, bf16[128,128]{1,0:T(8,128)(2,1)S(1)}, u32[]{:S(2)}, u32[]{:S(2)}) collective-permute-start(bf16[128,128]{1,0:T(8,128)(2,1)S(1)} %get-tuple-element.45), channel_id=1, source_target_pairs={{16,9},{17,10},{18,11},{19,12},{20,13},{21,14},{22,15},{23,8},{8,0... | collective-permute-start | bytes 98312 | tf_op jit(solution)/shard_map/ppermute | solution.py:148
  23.4 1.9 %collective-permute-start.6 = (bf16[128,128]{1,0:T(8,128)(2,1)S(1)}, bf16[128,128]{1,0:T(8,128)(2,1)S(1)}, u32[]{:S(2)}, u32[]{:S(2)}) collective-permute-start(bf16[128,128]{1,0:T(8,128)(2,1)S(1)} %get-tuple-element.46), channel_id=1, source_target_pairs={{16,12},{17,13},{18,14},{19,15},{20,8},{21,9},{22,10},{23,11},{8,0... | collective-permute-start | bytes 98312 | tf_op jit(solution)/shard_map/ppermute | solution.py:148
  23.5 2.2 %collective-permute-start.7 = (bf16[128,128]{1,0:T(8,128)(2,1)S(1)}, bf16[128,128]{1,0:T(8,128)(2,1)S(1)}, u32[]{:S(2)}, u32[]{:S(2)}) collective-permute-start(bf16[128,128]{1,0:T(8,128)(2,1)S(1)} %get-tuple-element.47), channel_id=1, source_target_pairs={{16,8},{17,9},{18,10},{19,11},{20,12},{21,13},{22,14},{23,15},{8,0... | collective-permute-start | bytes 98312 | tf_op jit(solution)/shard_map/ppermute | solution.py:148
  25.7 3.4 %copy-start.2 = (bf16[1,256,128,128]{3,2,1,0:T(8,128)(2,1)S(1)}, bf16[1,256,128,128]{3,2,1,0:T(8,128)(2,1)}, u32[]{:S(2)}) copy-start(bf16[1,256,128,128]{3,2,1,0:T(8,128)(2,1)} %param.7) | copy-start | bytes 25165828
  30.2 9.2 %collective-permute-start.8 = (bf16[128,128]{1,0:T(8,128)(2,1)S(1)}, bf16[128,128]{1,0:T(8,128)(2,1)S(1)}, u32[]{:S(2)}, u32[]{:S(2)}) collective-permute-start(bf16[128,128]{1,0:T(8,128)(2,1)S(1)} %get-tuple-element.48), channel_id=1, source_target_pairs={{8,7},{9,0},{10,1},{11,2},{12,3},{13,4},{14,5},{15,6},{0,16},{1,17... | collective-permute-start | bytes 98312 | tf_op jit(solution)/shard_map/ppermute | solution.py:148
  31.8 7.7 %collective-permute-start.9 = (bf16[128,128]{1,0:T(8,128)(2,1)S(1)}, bf16[128,128]{1,0:T(8,128)(2,1)S(1)}, u32[]{:S(2)}, u32[]{:S(2)}) collective-permute-start(bf16[128,128]{1,0:T(8,128)(2,1)S(1)} %get-tuple-element.49), channel_id=1, source_target_pairs={{8,1},{9,2},{10,3},{11,4},{12,5},{13,6},{14,7},{15,0},{0,16},{1,17... | collective-permute-start | bytes 98312 | tf_op jit(solution)/shard_map/ppermute | solution.py:148
  32.5 8.5 %collective-permute-start.10 = (bf16[128,128]{1,0:T(8,128)(2,1)S(1)}, bf16[128,128]{1,0:T(8,128)(2,1)S(1)}, u32[]{:S(2)}, u32[]{:S(2)}) collective-permute-start(bf16[128,128]{1,0:T(8,128)(2,1)S(1)} %get-tuple-element.50), channel_id=1, source_target_pairs={{8,4},{9,5},{10,6},{11,7},{12,0},{13,1},{14,2},{15,3},{0,16},{1,17... | collective-permute-start | bytes 98312 | tf_op jit(solution)/shard_map/ppermute | solution.py:148
  39.4 1.9 %collective-permute-start.11 = (bf16[128,128]{1,0:T(8,128)(2,1)S(1)}, bf16[128,128]{1,0:T(8,128)(2,1)S(1)}, u32[]{:S(2)}, u32[]{:S(2)}) collective-permute-start(bf16[128,128]{1,0:T(8,128)(2,1)S(1)} %get-tuple-element.51), channel_id=1, source_target_pairs={{8,0},{9,1},{10,2},{11,3},{12,4},{13,5},{14,6},{15,7},{0,16},{1,17... | collective-permute-start | bytes 98312 | tf_op jit(solution)/shard_map/ppermute | solution.py:148
  41.3 3.4 %copy-start.3 = (bf16[1,256,128,128]{3,2,1,0:T(8,128)(2,1)S(1)}, bf16[1,256,128,128]{3,2,1,0:T(8,128)(2,1)}, u32[]{:S(2)}) copy-start(bf16[1,256,128,128]{3,2,1,0:T(8,128)(2,1)} %param.7) | copy-start | bytes 25165828
  48.6 2.3 %collective-permute-start.12 = (bf16[128,128]{1,0:T(8,128)(2,1)S(1)}, bf16[128,128]{1,0:T(8,128)(2,1)S(1)}, u32[]{:S(2)}, u32[]{:S(2)}) collective-permute-start(bf16[128,128]{1,0:T(8,128)(2,1)S(1)} %get-tuple-element.52), channel_id=1, source_target_pairs={{0,31},{1,24},{2,25},{3,26},{4,27},{5,28},{6,29},{7,30},{24,16},{2... | collective-permute-start | bytes 98312 | tf_op jit(solution)/shard_map/ppermute | solution.py:148
  48.6 2.3 %collective-permute-start.13 = (bf16[128,128]{1,0:T(8,128)(2,1)S(1)}, bf16[128,128]{1,0:T(8,128)(2,1)S(1)}, u32[]{:S(2)}, u32[]{:S(2)}) collective-permute-start(bf16[128,128]{1,0:T(8,128)(2,1)S(1)} %get-tuple-element.53), channel_id=1, source_target_pairs={{0,25},{1,26},{2,27},{3,28},{4,29},{5,30},{6,31},{7,24},{24,16},{2... | collective-permute-start | bytes 98312 | tf_op jit(solution)/shard_map/ppermute | solution.py:148
  48.6 2.3 %collective-permute-start.14 = (bf16[128,128]{1,0:T(8,128)(2,1)S(1)}, bf16[128,128]{1,0:T(8,128)(2,1)S(1)}, u32[]{:S(2)}, u32[]{:S(2)}) collective-permute-start(bf16[128,128]{1,0:T(8,128)(2,1)S(1)} %get-tuple-element.54), channel_id=1, source_target_pairs={{0,28},{1,29},{2,30},{3,31},{4,24},{5,25},{6,26},{7,27},{24,16},{2... | collective-permute-start | bytes 98312 | tf_op jit(solution)/shard_map/ppermute | solution.py:148
  48.6 3.8 %collective-permute-start.15 = (bf16[128,128]{1,0:T(8,128)(2,1)S(1)}, bf16[128,128]{1,0:T(8,128)(2,1)S(1)}, u32[]{:S(2)}, u32[]{:S(2)}) collective-permute-start(bf16[128,128]{1,0:T(8,128)(2,1)S(1)} %get-tuple-element.55), channel_id=1, source_target_pairs={{0,24},{1,25},{2,26},{3,27},{4,28},{5,29},{6,30},{7,31},{24,16},{2... | collective-permute-start | bytes 98312 | tf_op jit(solution)/shard_map/ppermute | solution.py:148
  52.5 3.4 %copy-start.4 = (bf16[1,256,128,128]{3,2,1,0:T(8,128)(2,1)S(1)}, bf16[1,256,128,128]{3,2,1,0:T(8,128)(2,1)}, u32[]{:S(2)}) copy-start(bf16[1,256,128,128]{3,2,1,0:T(8,128)(2,1)} %param.7) | copy-start | bytes 25165828
  57.0 4.4 %collective-permute-start.16 = (bf16[128,128]{1,0:T(8,128)(2,1)S(1)}, bf16[128,128]{1,0:T(8,128)(2,1)S(1)}, u32[]{:S(2)}, u32[]{:S(2)}) collective-permute-start(bf16[128,128]{1,0:T(8,128)(2,1)S(1)} %get-tuple-element.56), channel_id=1, source_target_pairs={{24,23},{25,16},{26,17},{27,18},{28,19},{29,20},{30,21},{31,22},{1... | collective-permute-start | bytes 98312 | tf_op jit(solution)/shard_map/ppermute | solution.py:148
  57.7 4.5 %collective-permute-start.17 = (bf16[128,128]{1,0:T(8,128)(2,1)S(1)}, bf16[128,128]{1,0:T(8,128)(2,1)S(1)}, u32[]{:S(2)}, u32[]{:S(2)}) collective-permute-start(bf16[128,128]{1,0:T(8,128)(2,1)S(1)} %get-tuple-element.57), channel_id=1, source_target_pairs={{24,17},{25,18},{26,19},{27,20},{28,21},{29,22},{30,23},{31,16},{1... | collective-permute-start | bytes 98312 | tf_op jit(solution)/shard_map/ppermute | solution.py:148
  61.4 3.9 %collective-permute-start.18 = (bf16[128,128]{1,0:T(8,128)(2,1)S(1)}, bf16[128,128]{1,0:T(8,128)(2,1)S(1)}, u32[]{:S(2)}, u32[]{:S(2)}) collective-permute-start(bf16[128,128]{1,0:T(8,128)(2,1)S(1)} %get-tuple-element.58), channel_id=1, source_target_pairs={{24,20},{25,21},{26,22},{27,23},{28,16},{29,17},{30,18},{31,19},{1... | collective-permute-start | bytes 98312 | tf_op jit(solution)/shard_map/ppermute | solution.py:148
  61.4 4.2 %collective-permute-start.19 = (bf16[128,128]{1,0:T(8,128)(2,1)S(1)}, bf16[128,128]{1,0:T(8,128)(2,1)S(1)}, u32[]{:S(2)}, u32[]{:S(2)}) collective-permute-start(bf16[128,128]{1,0:T(8,128)(2,1)S(1)} %get-tuple-element.59), channel_id=1, source_target_pairs={{24,16},{25,17},{26,18},{27,19},{28,20},{29,21},{30,22},{31,23},{1... | collective-permute-start | bytes 98312 | tf_op jit(solution)/shard_map/ppermute | solution.py:148
  65.7 3.4 %copy-start.5 = (bf16[1,256,128,128]{3,2,1,0:T(8,128)(2,1)S(1)}, bf16[1,256,128,128]{3,2,1,0:T(8,128)(2,1)}, u32[]{:S(2)}) copy-start(bf16[1,256,128,128]{3,2,1,0:T(8,128)(2,1)} %param.7) | copy-start | bytes 25165828
  69.6 1.7 %collective-permute-start.20 = (bf16[128,128]{1,0:T(8,128)(2,1)S(1)}, bf16[128,128]{1,0:T(8,128)(2,1)S(1)}, u32[]{:S(2)}, u32[]{:S(2)}) collective-permute-start(bf16[128,128]{1,0:T(8,128)(2,1)S(1)} %get-tuple-element.60), channel_id=1, source_target_pairs={{16,15},{17,8},{18,9},{19,10},{20,11},{21,12},{22,13},{23,14},{8,0... | collective-permute-start | bytes 98312 | tf_op jit(solution)/shard_map/ppermute | solution.py:148
  69.7 2.1 %collective-permute-start.21 = (bf16[128,128]{1,0:T(8,128)(2,1)S(1)}, bf16[128,128]{1,0:T(8,128)(2,1)S(1)}, u32[]{:S(2)}, u32[]{:S(2)}) collective-permute-start(bf16[128,128]{1,0:T(8,128)(2,1)S(1)} %get-tuple-element.61), channel_id=1, source_target_pairs={{16,9},{17,10},{18,11},{19,12},{20,13},{21,14},{22,15},{23,8},{8,0... | collective-permute-start | bytes 98312 | tf_op jit(solution)/shard_map/ppermute | solution.py:148
  70.2 1.9 %collective-permute-start.22 = (bf16[128,128]{1,0:T(8,128)(2,1)S(1)}, bf16[128,128]{1,0:T(8,128)(2,1)S(1)}, u32[]{:S(2)}, u32[]{:S(2)}) collective-permute-start(bf16[128,128]{1,0:T(8,128)(2,1)S(1)} %get-tuple-element.62), channel_id=1, source_target_pairs={{16,12},{17,13},{18,14},{19,15},{20,8},{21,9},{22,10},{23,11},{8,0... | collective-permute-start | bytes 98312 | tf_op jit(solution)/shard_map/ppermute | solution.py:148
  70.3 2.1 %collective-permute-start.23 = (bf16[128,128]{1,0:T(8,128)(2,1)S(1)}, bf16[128,128]{1,0:T(8,128)(2,1)S(1)}, u32[]{:S(2)}, u32[]{:S(2)}) collective-permute-start(bf16[128,128]{1,0:T(8,128)(2,1)S(1)} %get-tuple-element.63), channel_id=1, source_target_pairs={{16,8},{17,9},{18,10},{19,11},{20,12},{21,13},{22,14},{23,15},{8,0... | collective-permute-start | bytes 98312 | tf_op jit(solution)/shard_map/ppermute | solution.py:148
  73.0 9.3 %collective-permute-start.24 = (bf16[128,128]{1,0:T(8,128)(2,1)S(1)}, bf16[128,128]{1,0:T(8,128)(2,1)S(1)}, u32[]{:S(2)}, u32[]{:S(2)}) collective-permute-start(bf16[128,128]{1,0:T(8,128)(2,1)S(1)} %get-tuple-element.64), channel_id=1, source_target_pairs={{8,7},{9,0},{10,1},{11,2},{12,3},{13,4},{14,5},{15,6},{0,16},{1,17... | collective-permute-start | bytes 98312 | tf_op jit(solution)/shard_map/ppermute | solution.py:148
  74.6 7.8 %collective-permute-start.25 = (bf16[128,128]{1,0:T(8,128)(2,1)S(1)}, bf16[128,128]{1,0:T(8,128)(2,1)S(1)}, u32[]{:S(2)}, u32[]{:S(2)}) collective-permute-start(bf16[128,128]{1,0:T(8,128)(2,1)S(1)} %get-tuple-element.65), channel_id=1, source_target_pairs={{8,1},{9,2},{10,3},{11,4},{12,5},{13,6},{14,7},{15,0},{0,16},{1,17... | collective-permute-start | bytes 98312 | tf_op jit(solution)/shard_map/ppermute | solution.py:148
  75.3 8.6 %collective-permute-start.26 = (bf16[128,128]{1,0:T(8,128)(2,1)S(1)}, bf16[128,128]{1,0:T(8,128)(2,1)S(1)}, u32[]{:S(2)}, u32[]{:S(2)}) collective-permute-start(bf16[128,128]{1,0:T(8,128)(2,1)S(1)} %get-tuple-element.66), channel_id=1, source_target_pairs={{8,4},{9,5},{10,6},{11,7},{12,0},{13,1},{14,2},{15,3},{0,16},{1,17... | collective-permute-start | bytes 98312 | tf_op jit(solution)/shard_map/ppermute | solution.py:148
  82.3 1.9 %collective-permute-start.27 = (bf16[128,128]{1,0:T(8,128)(2,1)S(1)}, bf16[128,128]{1,0:T(8,128)(2,1)S(1)}, u32[]{:S(2)}, u32[]{:S(2)}) collective-permute-start(bf16[128,128]{1,0:T(8,128)(2,1)S(1)} %get-tuple-element.67), channel_id=1, source_target_pairs={{8,0},{9,1},{10,2},{11,3},{12,4},{13,5},{14,6},{15,7},{0,16},{1,17... | collective-permute-start | bytes 98312 | tf_op jit(solution)/shard_map/ppermute | solution.py:148
  87.5 7.7 %collective-permute-start.31 = (f32[128,128]{1,0:T(8,128)S(1)}, f32[128,128]{1,0:T(8,128)S(1)}, u32[]{:S(2)}, u32[]{:S(2)}) collective-permute-start(f32[128,128]{1,0:T(8,128)S(1)} %select_select_fusion), channel_id=1, source_target_pairs={{0,8},{8,16},{16,24},{24,0},{1,9},{9,17},{17,25},{25,1},{2,10},{10... | collective-permute-start | bytes 196616 | tf_op jit(solution)/shard_map/ppermute | solution.py:155
  87.6 4.0 %collective-permute-start.28 = (bf16[128,128]{1,0:T(8,128)(2,1)S(1)}, bf16[128,128]{1,0:T(8,128)(2,1)S(1)}, u32[]{:S(2)}, u32[]{:S(2)}) collective-permute-start(bf16[128,128]{1,0:T(8,128)(2,1)S(1)} %get-tuple-element.69), channel_id=1, source_target_pairs={{0,7},{1,0},{2,1},{3,2},{4,3},{5,4},{6,5},{7,6},{8,15},{9,8},{10,9... | collective-permute-start | bytes 98312 | tf_op jit(solution)/shard_map/ppermute | solution.py:159
  88.6 6.6 %collective-permute-start.29 = (bf16[128,128]{1,0:T(8,128)(2,1)S(1)}, bf16[128,128]{1,0:T(8,128)(2,1)S(1)}, u32[]{:S(2)}, u32[]{:S(2)}) collective-permute-start(bf16[128,128]{1,0:T(8,128)(2,1)S(1)} %get-tuple-element.70), channel_id=1, source_target_pairs={{0,1},{1,2},{2,3},{3,4},{4,5},{5,6},{6,7},{7,0},{8,9},{9,10},{10,1... | collective-permute-start | bytes 98312 | tf_op jit(solution)/shard_map/ppermute | solution.py:159
  89.6 5.6 %collective-permute-start.30 = (bf16[128,128]{1,0:T(8,128)(2,1)S(1)}, bf16[128,128]{1,0:T(8,128)(2,1)S(1)}, u32[]{:S(2)}, u32[]{:S(2)}) collective-permute-start(bf16[128,128]{1,0:T(8,128)(2,1)S(1)} %get-tuple-element.71), channel_id=1, source_target_pairs={{0,4},{1,5},{2,6},{3,7},{4,0},{5,1},{6,2},{7,3},{8,12},{9,13},{10,... | collective-permute-start | bytes 98312 | tf_op jit(solution)/shard_map/ppermute | solution.py:159

commit v2 on v0

v2 whole, which is shorter than its diff:
```python
import functools

import jax
import jax.numpy as jnp
from jax import lax
from jax.experimental import pallas as pl
from jax.experimental.pallas import tpu as pltpu
from jax.sharding import PartitionSpec as P

SUB = 8
GROUP = 64
CHUNKS = 4
NT = (((1,), (1,)), ((), ()))
VMEM = pl.BlockSpec(memory_space=pltpu.VMEM)
SMEM = pl.BlockSpec(memory_space=pltpu.SMEM)
HBM = pl.BlockSpec(memory_space=pltpu.HBM)
LIVE, MONTH, NEAR, FAR = range(4)


def products(start, stop, table, tiles, x, acc):
    block = tiles.shape[-1]

    def round_of(g, carry):
        first = start + g * GROUP
        terms = []
        for u in range(0, GROUP, 2):
            s = first + u
            pair = jnp.concatenate([x[table[1, s]], x[table[1, s + 1]]], axis=0)
            both = tiles[pl.ds(s, 2)].reshape(2 * block, block)
            terms.append(
                lax.dot_general(pair.astype(jnp.bfloat16), both, NT, preferred_element_type=jnp.float32)
            )
        for u in range(0, GROUP, 2):
            s = first + u
            term = terms[u // 2]
            acc[table[0, s]] += term[:SUB, :block]
            acc[table[0, s + 1]] += term[SUB:, block:]
        return carry

    lax.fori_loop(0, (stop - start + GROUP - 1) // GROUP, round_of, 0)


def places(table, acc, own):
    nblk = acc.shape[0] - 1
    return table[2, FAR], table[2, NEAR], nblk // 2, 0


def clear(table, acc, own):
    for at in places(table, acc, own):
        acc[pl.ds(at, own)] = jnp.zeros((own,) + acc.shape[1:], acc.dtype)


def write_terms(table, acc, outs, own):
    for at, out in zip(places(table, acc, own), outs):
        out[...] = acc[pl.ds(at, own)].reshape(out.shape).astype(out.dtype)


def first_kernel(
    month, ncols, rows, cols, count, depth, forcing, tiles,
    o0, o1, o2, o3, kept, table, wet, force, x, acc, sems,
):
    own, width = depth.shape
    tracers, _, block = forcing.shape[1:]
    slots = tiles.shape[1]
    nblk = own * ncols
    size = slots // CHUNKS

    def load(i):
        part = pl.ds(i * size, size)
        return pltpu.make_async_copy(tiles.at[0, part], kept.at[part], sems.at[i])

    for i in range(CHUNKS):
        load(i).start()

    me = lax.axis_index("cols")
    my_month = lax.axis_index("month")
    live = count[0, 0]
    odd = lax.rem(me, 2) == 1
    table[2, LIVE] = live
    table[2, MONTH] = my_month
    table[2, NEAR] = jnp.where(odd, nblk - own, own)
    table[2, FAR] = jnp.where(odd, own, nblk - own)
    base = nblk - me * own

    def entry(s, carry):
        table[0, s] = jnp.where(s < live, lax.rem(rows[0, s] + base, nblk), nblk)
        table[1, s] = lax.rem(cols[0, s], own)
        return carry

    lax.fori_loop(0, slots, entry, 0, unroll=16)

    lane = lax.broadcasted_iota(jnp.int32, (width, block), 1)
    column = lax.broadcasted_iota(jnp.int32, (width, block), 0)
    spread = (lax.rem(lane, width) == column).astype(jnp.float32)
    below = jnp.dot(depth[...].astype(jnp.float32), spread, preferred_element_type=jnp.float32)
    level = lax.div(lax.broadcasted_iota(jnp.int32, (own, block), 1), width).astype(jnp.float32)
    wet[...] = jnp.broadcast_to((level < below).astype(jnp.float32)[:, None, :], wet.shape)
    force[...] = jnp.zeros_like(force)
    for t in range(tracers):
        force[:, t, :] = forcing[0, t]
    x[...] = force[...]
    clear(table, acc, own)

    for i in range(CHUNKS):
        load(i).wait()

        @pl.when((my_month == month) & (live > i * size))
        def _():
            products(i * size, jnp.minimum(live, (i + 1) * size), table, kept, x, acc)

    @pl.when(my_month == month)
    def _():
        write_terms(table, acc, (o0, o1, o2, o3), own)


def arrived_state(wet, arrived):
    total = arrived[0][...].astype(jnp.float32)
    for ref in arrived[1:]:
        total += ref[...].astype(jnp.float32)
    return total.reshape(wet.shape) * wet[...]


def step_kernel(month, table, wet, force, tiles, r0, r1, r2, r3, o0, o1, o2, o3, *refs):
    x, acc = refs[-2:]
    own = x.shape[0]

    @pl.when(table[2, MONTH] == month)
    def _():
        state = arrived_state(wet, (r0, r1, r2, r3))
        if len(refs) > 2:
            refs[0][...] = state
        x[...] = state + force[...]
        clear(table, acc, own)
        products(0, table[2, LIVE], table, tiles, x, acc)
        write_terms(table, acc, (o0, o1, o2, o3), own)


def last_kernel(table, wet, r0, r1, r2, r3, *refs):
    states, out = refs[:-1], refs[-1]
    month = table[2, MONTH]

    def put(state):
        for t in range(out.shape[1]):
            out[0, t] = state[:, t, :]

    for m, state in enumerate(states):

        @pl.when(month == m)
        def _():
            put(state[...])

    @pl.when(month == len(states))
    def _():
        put(arrived_state(wet, (r0, r1, r2, r3)))


def in_hbm(value):
    return pltpu.with_memory_space_constraint(value, pltpu.HBM)


def call(kernel, operands, in_specs, outs, out_specs, scratch):
    return pl.pallas_call(
        kernel,
        out_shape=outs,
        in_specs=in_specs,
        out_specs=out_specs,
        scratch_shapes=scratch,
        compiler_params=pltpu.CompilerParams(vmem_limit_bytes=12 * 2**20),
    )(*operands)


def idle_chain(active, months):
    to = (active - 1) % months
    if months != 4:
        return [(to - k) % months for k in range(1, months - 1)]
    if active ^ 1 == to:
        return [to ^ 2, to ^ 3]
    return [to ^ 1, active ^ 1]


def hops(active, months, ncols, move, whole):
    chain = [(active - 1) % months] + idle_chain(active, months) + [active]
    pairs = [(active * ncols + c, chain[0] * ncols + move(c)) for c in range(ncols)]
    if whole:
        for source, target in zip(chain, chain[1:]):
            pairs += [(source * ncols + c, target * ncols + c) for c in range(ncols)]
    return pairs


WHOLE = [True, True, True, True]
ORDER = [0, 1, 2, 3]


def on_device(forcing, tiles, tile_rows, tile_cols, tile_count, depth):
    months = lax.axis_size("month")
    ncols = lax.axis_size("cols")
    own, tracers, block = forcing.shape[1:]
    slots = tiles.shape[1]
    nblk = own * ncols
    far = lambda c: (c + 1) % ncols if c % 2 else (c - 1) % ncols
    near = lambda c: c ^ 1
    opposite = lambda c: (c + ncols // 2) % ncols
    moves = [far, near, opposite, lambda c: c]

    term = jax.ShapeDtypeStruct((own * SUB, block), jnp.bfloat16)
    plane = jax.ShapeDtypeStruct((own, SUB, block), jnp.float32)
    scratch = [
        pltpu.VMEM((own, SUB, block), jnp.float32),
        pltpu.VMEM((nblk + 1, SUB, block), jnp.float32),
    ]
    *terms, kept, table, wet, force = call(
        functools.partial(first_kernel, months - 1, ncols),
        (
            in_hbm(tile_rows),
            in_hbm(tile_cols),
            tile_count,
            in_hbm(depth),
            in_hbm(forcing.transpose(0, 2, 1, 3)),
            in_hbm(tiles),
        ),
        [SMEM, SMEM, SMEM, VMEM, VMEM, HBM],
        [term] * 4
        + [
            pltpu.VMEM(tiles.shape[1:], tiles.dtype),
            jax.ShapeDtypeStruct((3, slots), jnp.int32),
            plane,
            plane,
        ],
        [VMEM] * 5 + [SMEM, VMEM, VMEM],
        scratch + [pltpu.SemaphoreType.DMA((CHUNKS,))],
    )
    states = []
    for step in range(2 * months):
        month = months - 1 - step % months
        if step > 0:
            keep = step > months
            *terms, = call(
                functools.partial(step_kernel, month),
                (table, wet, force, kept, *arrived),
                [SMEM] + [VMEM] * 7,
                [term] * 4 + [plane] * keep,
                [VMEM] * (4 + keep),
                scratch,
            )
            if keep:
                states.insert(0, terms.pop())
        arrived = [None] * 4
        for k in ORDER:
            arrived[k] = lax.ppermute(
                terms[k], ("month", "cols"), hops(month, months, ncols, moves[k], WHOLE[k])
            )

    (held,) = call(
        last_kernel,
        (table, wet, *arrived, *states),
        [SMEM] + [VMEM] * (4 + months),
        [jax.ShapeDtypeStruct((1, tracers, own, block), jnp.float32)],
        [VMEM],
        [],
    )
    result = lax.ppermute(held, "month", [(m, (m + 1) % months) for m in range(months)])
    return result.transpose(0, 2, 1, 3)


def solution(mesh):
    in_specs = (
        P("month", "cols", None, None),
        P("month", "cols", None, None),
        P("month", "cols"),
        P("month", "cols"),
        P("month", "cols"),
        P("cols", None),
    )
    out_specs = P("month", "cols", None, None)
    return jax.shard_map(
        on_device, mesh=mesh, in_specs=in_specs, out_specs=out_specs, check_vma=False
    )
```

time: 826 us -> 72 us (0.09)
  waiting for transfers between devices: 708 us -> 22.8 us
  other arithmetic: 75.4 us -> 0 us
  starting transfers between devices: 0.79 us -> 35.5 us
  matrix products: 13.4 us -> 0 us
  between operations: 13.4 us -> 0.79 us
  Pallas kernels: 0 us -> 11.4 us
  local copies, waits for them, and re-layouts: 10.4 us -> 0.62 us
    reduce_scatter x8 -> x0, waiting for transfers between devices: 695 us -> none  [reduce_terms(): lax.psum_scatter(partial_terms.astype(jnp.bfloat16), 'cols', scatter_dime...]
    scatter-add x2 -> x0, other arithmetic: 50.8 us -> none  [place(): buffer.at[target].add(terms * inside.astype(jnp.float32)[:, None, None])]
    ppermute x8 -> x33, starting transfers between devices: 0.46 us -> 35.5 us  [the longest x32 34.3 us: on_device(): lax.ppermute(terms[k], ('month', 'cols'), hops(month, months, ncols, move...]
    convert_element_type x26 -> x0, other arithmetic: 15.5 us -> none  [the longest x8 14.1 us: reduce_terms(): partial_terms.astype(jnp.bfloat16)]
    dot_general x2 -> x0, matrix products: 13.4 us -> none  [compute(): jnp.einsum('stj,sij->sti', picked, plates, preferred_element_type=jnp.flo...]
    pallas_call x0 -> x9, Pallas kernels: none -> 11.4 us  [call(): pl.pallas_call(kernel, out_shape=outs, in_specs=in_specs, out_specs=out_s...]
    ppermute x8 -> x33, waiting for transfers between devices: 12.7 us -> 22.8 us  [the longest x32 18.6 us: on_device(): lax.ppermute(terms[k], ('month', 'cols'), hops(month, months, ncols, move...]
  transfers between devices with their start and end apart: 16 -> 33, of which waited for: 16 -> 21; matrix products, arithmetic and copies ran while one was open for 0% -> 0% of each run, Pallas kernels for 0% -> 0%
where the time goes in v2:
time: 72 us; the launch traced here: 71.1 us
  starting transfers between devices  35.5 us (49%)
  waiting for transfers between devices  22.8 us (32%)
  Pallas kernels  11.4 us (16%)
  between operations  0.79 us (1%)
    ppermute x32, starting transfers between devices, on_device(): lax.ppermute(terms[k], ('month', 'cols'), hops(month, months, ncols, move...  34.3 us
    ppermute x32, waiting for transfers between devices, on_device(): lax.ppermute(terms[k], ('month', 'cols'), hops(month, months, ncols, move...  18.6 us
    pallas_call x9, Pallas kernels, call(): pl.pallas_call(kernel, out_shape=outs, in_specs=in_specs, out_specs=out_s...  11.4 us
    ppermute x1, waiting for transfers between devices, on_device(): lax.ppermute(held, 'month', [(m, (m + 1) % months) for m in range(months)])  4.24 us
  transfers between devices with their start and end apart: 33, of which 21 were waited for; matrix products, arithmetic and copies ran while one was open for 0% of the time, Pallas kernels for 0%

profile of v2, /device:TPU:0, one launch (start us, length us, event | category | flops | bytes accessed | tf_op | source)
XLA Modules:
  0.0 71.1 jit_solution(11068391937577566518)
XLA Ops:
  0.7 5.0 %shard_map.64 = (bf16[128,128]{1,0:T(8,128)(2,1)S(1)}, bf16[128,128]{1,0:T(8,128)(2,1)S(1)}, bf16[128,128]{1,0:T(8,128)(2,1)S(1)}, bf16[128,128]{1,0:T(8,128)(2,...) custom-call(s32[1,256]{1,0:T(1,128)} %rows.1, ...), custom_call_target="tpu_custom_call" | custom-call | tf_op jit(solution)/shard_map/pallas_call | solution.py:162
  5.6 0.5 collective-permute-start
  6.2 2.1 %collective-permute-start.1 = (bf16[128,128]{1,0:T(8,128)(2,1)S(1)}, bf16[128,128]{1,0:T(8,128)(2,1)S(1)}, u32[]{:S(2)}, u32[]{:S(2)}) collective-permute-start(bf16[128,128]{1,0:T(8,128)(2,1)S(1)} %get-tuple-element.49), channel_id=1, source_target_pairs={{24,17},{25,16},{26,19},{27,18},{28,21},{29,20},{30,23},{31,22},{1... | collective-permute-start | bytes 98312 | tf_op jit(solution)/shard_map/ppermute | solution.py:249
  8.2 4.8 %collective-permute-start.2 = (bf16[128,128]{1,0:T(8,128)(2,1)S(1)}, bf16[128,128]{1,0:T(8,128)(2,1)S(1)}, u32[]{:S(2)}, u32[]{:S(2)}) collective-permute-start(bf16[128,128]{1,0:T(8,128)(2,1)S(1)} %get-tuple-element.50), channel_id=1, source_target_pairs={{24,20},{25,21},{26,22},{27,23},{28,16},{29,17},{30,18},{31,19},{1... | collective-permute-start | bytes 98312 | tf_op jit(solution)/shard_map/ppermute | solution.py:249
  13.1 0.8 %collective-permute-done.2.r2 = bf16[128,128]{1,0:T(8,128)(2,1)S(1)} collective-permute-done((bf16[128,128]{1,0:T(8,128)(2,1)S(1)}, bf16[128,128]{1,0:T(8,128)(2,1)S(1)}, u32[]{:S(2)}, u32[]{:S(2)}) %collective-permute-start.2) | collective-permute-done | bytes 32800 | tf_op jit(solution)/shard_map/ppermute | solution.py:249
  13.9 3.1 %collective-permute-done.3.r3 = bf16[128,128]{1,0:T(8,128)(2,1)S(1)} collective-permute-done((bf16[128,128]{1,0:T(8,128)(2,1)S(1)}, bf16[128,128]{1,0:T(8,128)(2,1)S(1)}, u32[]{:S(2)}, u32[]{:S(2)}) %collective-permute-start.3) | collective-permute-done | bytes 32800 | tf_op jit(solution)/shard_map/ppermute | solution.py:249
  17.0 0.6 shard_map.65
  17.6 0.5 collective-permute-start.5
  18.3 0.9 %collective-permute-done.4.r0 = bf16[128,128]{1,0:T(8,128)(2,1)S(1)} collective-permute-done((bf16[128,128]{1,0:T(8,128)(2,1)S(1)}, bf16[128,128]{1,0:T(8,128)(2,1)S(1)}, u32[]{:S(2)}, u32[]{:S(2)}) %collective-permute-start.4) | collective-permute-done | bytes 32800 | tf_op jit(solution)/shard_map/ppermute | solution.py:249
  19.2 0.5 collective-permute-done.5.r1
  20.1 0.3 collective-permute-done.7.r3
  20.4 0.6 shard_map.66
  21.0 1.6 %collective-permute-start.8 = (bf16[128,128]{1,0:T(8,128)(2,1)S(1)}, bf16[128,128]{1,0:T(8,128)(2,1)S(1)}, u32[]{:S(2)}, u32[]{:S(2)}) collective-permute-start(bf16[128,128]{1,0:T(8,128)(2,1)S(1)} %get-tuple-element.56), channel_id=1, source_target_pairs={{8,7},{9,2},{10,1},{11,4},{12,3},{13,6},{14,5},{15,0},{0,16},{1,17... | collective-permute-start | bytes 98312 | tf_op jit(solution)/shard_map/ppermute | solution.py:249
  22.6 0.7 collective-permute-start.9
  23.3 5.2 %collective-permute-start.10 = (bf16[128,128]{1,0:T(8,128)(2,1)S(1)}, bf16[128,128]{1,0:T(8,128)(2,1)S(1)}, u32[]{:S(2)}, u32[]{:S(2)}) collective-permute-start(bf16[128,128]{1,0:T(8,128)(2,1)S(1)} %get-tuple-element.58), channel_id=1, source_target_pairs={{8,4},{9,5},{10,6},{11,7},{12,0},{13,1},{14,2},{15,3},{0,16},{1,17... | collective-permute-start | bytes 98312 | tf_op jit(solution)/shard_map/ppermute | solution.py:249
  28.6 1.5 %collective-permute-done.10.r2 = bf16[128,128]{1,0:T(8,128)(2,1)S(1)} collective-permute-done((bf16[128,128]{1,0:T(8,128)(2,1)S(1)}, bf16[128,128]{1,0:T(8,128)(2,1)S(1)}, u32[]{:S(2)}, u32[]{:S(2)}) %collective-permute-start.10) | collective-permute-done | bytes 32800 | tf_op jit(solution)/shard_map/ppermute | solution.py:249
  30.4 1.3 %shard_map.67 = (bf16[128,128]{1,0:T(8,128)(2,1)S(1)}, bf16[128,128]{1,0:T(8,128)(2,1)S(1)}, bf16[128,128]{1,0:T(8,128)(2,1)S(1)}, bf16[128,128]{1,0:T(8,128)(2,1)S(1)}) custom-call(s32[3,256]{1,0:T(4,128)S(1)} %get-tuple-element.44.table, f32[16,8,128]{2,1,0:T(8,128)S(1)} %get-tuple-element.45.wet, f32[16,8,128]{2,1,0:T(8,128)S(1)} %get-tuple-element.46.force, ...), custom_call_target="tpu_custom_call" | custom-call | tf_op jit(solution)/shard_map/pallas_call | solution.py:162
  31.9 1.7 %collective-permute-start.14 = (bf16[128,128]{1,0:T(8,128)(2,1)S(1)}, bf16[128,128]{1,0:T(8,128)(2,1)S(1)}, u32[]{:S(2)}, u32[]{:S(2)}) collective-permute-start(bf16[128,128]{1,0:T(8,128)(2,1)S(1)} %get-tuple-element.62), channel_id=1, source_target_pairs={{0,28},{1,29},{2,30},{3,31},{4,24},{5,25},{6,26},{7,27},{24,16},{2... | collective-permute-start | bytes 98312 | tf_op jit(solution)/shard_map/ppermute | solution.py:249
  33.6 0.5 collective-permute-start.15
  34.1 1.1 %collective-permute-done.14.r2 = bf16[128,128]{1,0:T(8,128)(2,1)S(1)} collective-permute-done((bf16[128,128]{1,0:T(8,128)(2,1)S(1)}, bf16[128,128]{1,0:T(8,128)(2,1)S(1)}, u32[]{:S(2)}, u32[]{:S(2)}) %collective-permute-start.14) | collective-permute-done | bytes 32800 | tf_op jit(solution)/shard_map/ppermute | solution.py:249
  35.2 0.5 collective-permute-done.15.r3
  35.7 0.6 shard_map.68
  36.3 0.8 %collective-permute-start.16 = (bf16[128,128]{1,0:T(8,128)(2,1)S(1)}, bf16[128,128]{1,0:T(8,128)(2,1)S(1)}, u32[]{:S(2)}, u32[]{:S(2)}) collective-permute-start(bf16[128,128]{1,0:T(8,128)(2,1)S(1)} %get-tuple-element.64), channel_id=1, source_target_pairs={{24,23},{25,18},{26,17},{27,20},{28,19},{29,22},{30,21},{31,16},{1... | collective-permute-start | bytes 98312 | tf_op jit(solution)/shard_map/ppermute | solution.py:249
  37.0 3.6 %collective-permute-start.17 = (bf16[128,128]{1,0:T(8,128)(2,1)S(1)}, bf16[128,128]{1,0:T(8,128)(2,1)S(1)}, u32[]{:S(2)}, u32[]{:S(2)}) collective-permute-start(bf16[128,128]{1,0:T(8,128)(2,1)S(1)} %get-tuple-element.65), channel_id=1, source_target_pairs={{24,17},{25,16},{26,19},{27,18},{28,21},{29,20},{30,23},{31,22},{1... | collective-permute-start | bytes 98312 | tf_op jit(solution)/shard_map/ppermute | solution.py:249
  40.6 0.3 collective-permute-start.18
  41.0 0.5 collective-permute-done.17.r1
  41.5 3.1 %collective-permute-done.18.r2 = bf16[128,128]{1,0:T(8,128)(2,1)S(1)} collective-permute-done((bf16[128,128]{1,0:T(8,128)(2,1)S(1)}, bf16[128,128]{1,0:T(8,128)(2,1)S(1)}, u32[]{:S(2)}, u32[]{:S(2)}) %collective-permute-start.18) | collective-permute-done | bytes 32800 | tf_op jit(solution)/shard_map/ppermute | solution.py:249
  44.6 0.4 collective-permute-done.19.r3
  44.9 0.6 shard_map.69
  45.6 2.6 %collective-permute-start.21 = (bf16[128,128]{1,0:T(8,128)(2,1)S(1)}, bf16[128,128]{1,0:T(8,128)(2,1)S(1)}, u32[]{:S(2)}, u32[]{:S(2)}) collective-permute-start(bf16[128,128]{1,0:T(8,128)(2,1)S(1)} %get-tuple-element.69), channel_id=1, source_target_pairs={{16,9},{17,8},{18,11},{19,10},{20,13},{21,12},{22,15},{23,14},{8,0... | collective-permute-start | bytes 98312 | tf_op jit(solution)/shard_map/ppermute | solution.py:249
  48.2 0.8 %collective-permute-start.22 = (bf16[128,128]{1,0:T(8,128)(2,1)S(1)}, bf16[128,128]{1,0:T(8,128)(2,1)S(1)}, u32[]{:S(2)}, u32[]{:S(2)}) collective-permute-start(bf16[128,128]{1,0:T(8,128)(2,1)S(1)} %get-tuple-element.70), channel_id=1, source_target_pairs={{16,12},{17,13},{18,14},{19,15},{20,8},{21,9},{22,10},{23,11},{8,0... | collective-permute-start | bytes 98312 | tf_op jit(solution)/shard_map/ppermute | solution.py:249
  49.0 0.8 %collective-permute-done.21.r1 = bf16[128,128]{1,0:T(8,128)(2,1)S(1)} collective-permute-done((bf16[128,128]{1,0:T(8,128)(2,1)S(1)}, bf16[128,128]{1,0:T(8,128)(2,1)S(1)}, u32[]{:S(2)}, u32[]{:S(2)}) %collective-permute-start.21) | collective-permute-done | bytes 32800 | tf_op jit(solution)/shard_map/ppermute | solution.py:249
  49.8 0.8 %collective-permute-done.22.r2 = bf16[128,128]{1,0:T(8,128)(2,1)S(1)} collective-permute-done((bf16[128,128]{1,0:T(8,128)(2,1)S(1)}, bf16[128,128]{1,0:T(8,128)(2,1)S(1)}, u32[]{:S(2)}, u32[]{:S(2)}) %collective-permute-start.22) | collective-permute-done | bytes 32800 | tf_op jit(solution)/shard_map/ppermute | solution.py:249
  50.9 0.6 shard_map.70
  51.5 1.1 %collective-permute-start.24 = (bf16[128,128]{1,0:T(8,128)(2,1)S(1)}, bf16[128,128]{1,0:T(8,128)(2,1)S(1)}, u32[]{:S(2)}, u32[]{:S(2)}) collective-permute-start(bf16[128,128]{1,0:T(8,128)(2,1)S(1)} %get-tuple-element.72), channel_id=1, source_target_pairs={{8,7},{9,2},{10,1},{11,4},{12,3},{13,6},{14,5},{15,0},{0,16},{1,17... | collective-permute-start | bytes 98312 | tf_op jit(solution)/shard_map/ppermute | solution.py:249
  52.6 1.1 %collective-permute-start.25 = (bf16[128,128]{1,0:T(8,128)(2,1)S(1)}, bf16[128,128]{1,0:T(8,128)(2,1)S(1)}, u32[]{:S(2)}, u32[]{:S(2)}) collective-permute-start(bf16[128,128]{1,0:T(8,128)(2,1)S(1)} %get-tuple-element.73), channel_id=1, source_target_pairs={{8,1},{9,0},{10,3},{11,2},{12,5},{13,4},{14,7},{15,6},{0,16},{1,17... | collective-permute-start | bytes 98312 | tf_op jit(solution)/shard_map/ppermute | solution.py:249
  53.8 3.5 %collective-permute-start.26 = (bf16[128,128]{1,0:T(8,128)(2,1)S(1)}, bf16[128,128]{1,0:T(8,128)(2,1)S(1)}, u32[]{:S(2)}, u32[]{:S(2)}) collective-permute-start(bf16[128,128]{1,0:T(8,128)(2,1)S(1)} %get-tuple-element.74), channel_id=1, source_target_pairs={{8,4},{9,5},{10,6},{11,7},{12,0},{13,1},{14,2},{15,3},{0,16},{1,17... | collective-permute-start | bytes 98312 | tf_op jit(solution)/shard_map/ppermute | solution.py:249
  57.3 1.8 %collective-permute-done.24.r0 = bf16[128,128]{1,0:T(8,128)(2,1)S(1)} collective-permute-done((bf16[128,128]{1,0:T(8,128)(2,1)S(1)}, bf16[128,128]{1,0:T(8,128)(2,1)S(1)}, u32[]{:S(2)}, u32[]{:S(2)}) %collective-permute-start.24) | collective-permute-done | bytes 32800 | tf_op jit(solution)/shard_map/ppermute | solution.py:249
  59.2 1.4 %shard_map.71 = (bf16[128,128]{1,0:T(8,128)(2,1)S(1)}, bf16[128,128]{1,0:T(8,128)(2,1)S(1)}, bf16[128,128]{1,0:T(8,128)(2,1)S(1)}, bf16[128,128]{1,0:T(8,128)(2,1)S(1)}, f32[16,8,128]{2,1,0:T(8,128)S(1)}) custom-call(s32[3,256]{1,0:T(4,128)S(1)} %get-tuple-element.44.table, f32[16,8,128]{2,1,0:T(8,128)S(1)} %get-tuple-element.45.wet, ...), custom_call_target="tpu_custom_call" | custom-call | tf_op jit(solution)/shard_map/pallas_call | solution.py:162
  60.5 0.8 %collective-permute-start.28 = (bf16[128,128]{1,0:T(8,128)(2,1)S(1)}, bf16[128,128]{1,0:T(8,128)(2,1)S(1)}, u32[]{:S(2)}, u32[]{:S(2)}) collective-permute-start(bf16[128,128]{1,0:T(8,128)(2,1)S(1)} %get-tuple-element.76), channel_id=1, source_target_pairs={{0,31},{1,26},{2,25},{3,28},{4,27},{5,30},{6,29},{7,24},{24,16},{2... | collective-permute-start | bytes 98312 | tf_op jit(solution)/shard_map/ppermute | solution.py:249
  61.3 0.5 collective-permute-start.30
  61.8 1.0 %collective-permute-start.31 = (bf16[128,128]{1,0:T(8,128)(2,1)S(1)}, bf16[128,128]{1,0:T(8,128)(2,1)S(1)}, u32[]{:S(2)}, u32[]{:S(2)}) collective-permute-start(bf16[128,128]{1,0:T(8,128)(2,1)S(1)} %get-tuple-element.79), channel_id=1, source_target_pairs={{0,24},{1,25},{2,26},{3,27},{4,28},{5,29},{6,30},{7,31},{24,16},{2... | collective-permute-start | bytes 98312 | tf_op jit(solution)/shard_map/ppermute | solution.py:249
  62.9 0.5 collective-permute-done.30.r2
  63.4 1.0 %collective-permute-done.31.r3 = bf16[128,128]{1,0:T(8,128)(2,1)S(1)} collective-permute-done((bf16[128,128]{1,0:T(8,128)(2,1)S(1)}, bf16[128,128]{1,0:T(8,128)(2,1)S(1)}, u32[]{:S(2)}, u32[]{:S(2)}) %collective-permute-start.31) | collective-permute-done | bytes 32800 | tf_op jit(solution)/shard_map/ppermute | solution.py:249
  64.4 0.6 shard_map.72
  65.1 1.2 %collective-permute-start.32 = (f32[1,6,16,128]{3,2,1,0:T(8,128)S(1)}, f32[1,6,16,128]{3,2,1,0:T(8,128)S(1)}, u32[]{:S(2)}, u32[]{:S(2)}) collective-permute-start(f32[1,6,16,128]{3,2,1,0:T(8,128)S(1)} %shard_map.72), channel_id=1, source_target_pairs={{0,8},{8,16},{16,24},{24,0},{1,9},{9,17},{17,25},{25,1},{2,10},{10... | collective-permute-start | bytes 147464 | tf_op jit(solution)/shard_map/ppermute | solution.py:261
  66.2 4.2 %collective-permute-done.32 = f32[1,6,16,128]{3,2,1,0:T(8,128)S(1)} collective-permute-done((f32[1,6,16,128]{3,2,1,0:T(8,128)S(1)}, f32[1,6,16,128]{3,2,1,0:T(8,128)S(1)}, u32[]{:S(2)}, u32[]{:S(2)}) %collective-permute-start.32) | collective-permute-done | bytes 49184 | tf_op jit(solution)/shard_map/ppermute | solution.py:261
  70.5 0.6 copy.9
  (28 shorter events, 1.7 us)
Async XLA Ops:
  5.6 7.4 %collective-permute-start = (bf16[128,128]{1,0:T(8,128)(2,1)S(1)}, bf16[128,128]{1,0:T(8,128)(2,1)S(1)}, u32[]{:S(2)}, u32[]{:S(2)}) collective-permute-start(bf16[128,128]{1,0:T(8,128)(2,1)S(1)} %get-tuple-element.48), channel_id=1, source_target_pairs={{24,23},{25,18},{26,17},{27,20},{28,19},{29,22},{30,21},{31,16},{1... | collective-permute-start | bytes 98312 | tf_op jit(solution)/shard_map/ppermute | solution.py:249
  6.2 6.9 %collective-permute-start.1 = (bf16[128,128]{1,0:T(8,128)(2,1)S(1)}, bf16[128,128]{1,0:T(8,128)(2,1)S(1)}, u32[]{:S(2)}, u32[]{:S(2)}) collective-permute-start(bf16[128,128]{1,0:T(8,128)(2,1)S(1)} %get-tuple-element.49), channel_id=1, source_target_pairs={{24,17},{25,16},{26,19},{27,18},{28,21},{29,20},{30,23},{31,22},{1... | collective-permute-start | bytes 98312 | tf_op jit(solution)/shard_map/ppermute | solution.py:249
  8.2 5.7 %collective-permute-start.2 = (bf16[128,128]{1,0:T(8,128)(2,1)S(1)}, bf16[128,128]{1,0:T(8,128)(2,1)S(1)}, u32[]{:S(2)}, u32[]{:S(2)}) collective-permute-start(bf16[128,128]{1,0:T(8,128)(2,1)S(1)} %get-tuple-element.50), channel_id=1, source_target_pairs={{24,20},{25,21},{26,22},{27,23},{28,16},{29,17},{30,18},{31,19},{1... | collective-permute-start | bytes 98312 | tf_op jit(solution)/shard_map/ppermute | solution.py:249
  13.0 3.9 %collective-permute-start.3 = (bf16[128,128]{1,0:T(8,128)(2,1)S(1)}, bf16[128,128]{1,0:T(8,128)(2,1)S(1)}, u32[]{:S(2)}, u32[]{:S(2)}) collective-permute-start(bf16[128,128]{1,0:T(8,128)(2,1)S(1)} %get-tuple-element.51), channel_id=1, source_target_pairs={{24,16},{25,17},{26,18},{27,19},{28,20},{29,21},{30,22},{31,23},{1... | collective-permute-start | bytes 98312 | tf_op jit(solution)/shard_map/ppermute | solution.py:249
  17.6 1.7 %collective-permute-start.4 = (bf16[128,128]{1,0:T(8,128)(2,1)S(1)}, bf16[128,128]{1,0:T(8,128)(2,1)S(1)}, u32[]{:S(2)}, u32[]{:S(2)}) collective-permute-start(bf16[128,128]{1,0:T(8,128)(2,1)S(1)} %get-tuple-element.52), channel_id=1, source_target_pairs={{16,15},{17,10},{18,9},{19,12},{20,11},{21,14},{22,13},{23,8},{8,0... | collective-permute-start | bytes 98312 | tf_op jit(solution)/shard_map/ppermute | solution.py:249
  17.6 2.1 %collective-permute-start.5 = (bf16[128,128]{1,0:T(8,128)(2,1)S(1)}, bf16[128,128]{1,0:T(8,128)(2,1)S(1)}, u32[]{:S(2)}, u32[]{:S(2)}) collective-permute-start(bf16[128,128]{1,0:T(8,128)(2,1)S(1)} %get-tuple-element.53), channel_id=1, source_target_pairs={{16,9},{17,8},{18,11},{19,10},{20,13},{21,12},{22,15},{23,14},{8,0... | collective-permute-start | bytes 98312 | tf_op jit(solution)/shard_map/ppermute | solution.py:249
  18.2 1.9 %collective-permute-start.6 = (bf16[128,128]{1,0:T(8,128)(2,1)S(1)}, bf16[128,128]{1,0:T(8,128)(2,1)S(1)}, u32[]{:S(2)}, u32[]{:S(2)}) collective-permute-start(bf16[128,128]{1,0:T(8,128)(2,1)S(1)} %get-tuple-element.54), channel_id=1, source_target_pairs={{16,12},{17,13},{18,14},{19,15},{20,8},{21,9},{22,10},{23,11},{8,0... | collective-permute-start | bytes 98312 | tf_op jit(solution)/shard_map/ppermute | solution.py:249
  18.2 2.1 %collective-permute-start.7 = (bf16[128,128]{1,0:T(8,128)(2,1)S(1)}, bf16[128,128]{1,0:T(8,128)(2,1)S(1)}, u32[]{:S(2)}, u32[]{:S(2)}) collective-permute-start(bf16[128,128]{1,0:T(8,128)(2,1)S(1)} %get-tuple-element.55), channel_id=1, source_target_pairs={{16,8},{17,9},{18,10},{19,11},{20,12},{21,13},{22,14},{23,15},{8,0... | collective-permute-start | bytes 98312 | tf_op jit(solution)/shard_map/ppermute | solution.py:249
  21.0 7.6 %collective-permute-start.8 = (bf16[128,128]{1,0:T(8,128)(2,1)S(1)}, bf16[128,128]{1,0:T(8,128)(2,1)S(1)}, u32[]{:S(2)}, u32[]{:S(2)}) collective-permute-start(bf16[128,128]{1,0:T(8,128)(2,1)S(1)} %get-tuple-element.56), channel_id=1, source_target_pairs={{8,7},{9,2},{10,1},{11,4},{12,3},{13,6},{14,5},{15,0},{0,16},{1,17... | collective-permute-start | bytes 98312 | tf_op jit(solution)/shard_map/ppermute | solution.py:249
  22.6 6.0 %collective-permute-start.9 = (bf16[128,128]{1,0:T(8,128)(2,1)S(1)}, bf16[128,128]{1,0:T(8,128)(2,1)S(1)}, u32[]{:S(2)}, u32[]{:S(2)}) collective-permute-start(bf16[128,128]{1,0:T(8,128)(2,1)S(1)} %get-tuple-element.57), channel_id=1, source_target_pairs={{8,1},{9,0},{10,3},{11,2},{12,5},{13,4},{14,7},{15,6},{0,16},{1,17... | collective-permute-start | bytes 98312 | tf_op jit(solution)/shard_map/ppermute | solution.py:249
  23.3 6.8 %collective-permute-start.10 = (bf16[128,128]{1,0:T(8,128)(2,1)S(1)}, bf16[128,128]{1,0:T(8,128)(2,1)S(1)}, u32[]{:S(2)}, u32[]{:S(2)}) collective-permute-start(bf16[128,128]{1,0:T(8,128)(2,1)S(1)} %get-tuple-element.58), channel_id=1, source_target_pairs={{8,4},{9,5},{10,6},{11,7},{12,0},{13,1},{14,2},{15,3},{0,16},{1,17... | collective-permute-start | bytes 98312 | tf_op jit(solution)/shard_map/ppermute | solution.py:249
  28.5 1.9 %collective-permute-start.11 = (bf16[128,128]{1,0:T(8,128)(2,1)S(1)}, bf16[128,128]{1,0:T(8,128)(2,1)S(1)}, u32[]{:S(2)}, u32[]{:S(2)}) collective-permute-start(bf16[128,128]{1,0:T(8,128)(2,1)S(1)} %get-tuple-element.59), channel_id=1, source_target_pairs={{8,0},{9,1},{10,2},{11,3},{12,4},{13,5},{14,6},{15,7},{0,16},{1,17... | collective-permute-start | bytes 98312 | tf_op jit(solution)/shard_map/ppermute | solution.py:249
  31.8 2.3 %collective-permute-start.12 = (bf16[128,128]{1,0:T(8,128)(2,1)S(1)}, bf16[128,128]{1,0:T(8,128)(2,1)S(1)}, u32[]{:S(2)}, u32[]{:S(2)}) collective-permute-start(bf16[128,128]{1,0:T(8,128)(2,1)S(1)} %get-tuple-element.60), channel_id=1, source_target_pairs={{0,31},{1,26},{2,25},{3,28},{4,27},{5,30},{6,29},{7,24},{24,16},{2... | collective-permute-start | bytes 98312 | tf_op jit(solution)/shard_map/ppermute | solution.py:249
  31.8 2.2 %collective-permute-start.13 = (bf16[128,128]{1,0:T(8,128)(2,1)S(1)}, bf16[128,128]{1,0:T(8,128)(2,1)S(1)}, u32[]{:S(2)}, u32[]{:S(2)}) collective-permute-start(bf16[128,128]{1,0:T(8,128)(2,1)S(1)} %get-tuple-element.61), channel_id=1, source_target_pairs={{0,25},{1,24},{2,27},{3,26},{4,29},{5,28},{6,31},{7,30},{24,16},{2... | collective-permute-start | bytes 98312 | tf_op jit(solution)/shard_map/ppermute | solution.py:249
  31.9 3.3 %collective-permute-start.14 = (bf16[128,128]{1,0:T(8,128)(2,1)S(1)}, bf16[128,128]{1,0:T(8,128)(2,1)S(1)}, u32[]{:S(2)}, u32[]{:S(2)}) collective-permute-start(bf16[128,128]{1,0:T(8,128)(2,1)S(1)} %get-tuple-element.62), channel_id=1, source_target_pairs={{0,28},{1,29},{2,30},{3,31},{4,24},{5,25},{6,26},{7,27},{24,16},{2... | collective-permute-start | bytes 98312 | tf_op jit(solution)/shard_map/ppermute | solution.py:249
  33.6 2.1 %collective-permute-start.15 = (bf16[128,128]{1,0:T(8,128)(2,1)S(1)}, bf16[128,128]{1,0:T(8,128)(2,1)S(1)}, u32[]{:S(2)}, u32[]{:S(2)}) collective-permute-start(bf16[128,128]{1,0:T(8,128)(2,1)S(1)} %get-tuple-element.63), channel_id=1, source_target_pairs={{0,24},{1,25},{2,26},{3,27},{4,28},{5,29},{6,30},{7,31},{24,16},{2... | collective-permute-start | bytes 98312 | tf_op jit(solution)/shard_map/ppermute | solution.py:249
  36.3 4.7 %collective-permute-start.16 = (bf16[128,128]{1,0:T(8,128)(2,1)S(1)}, bf16[128,128]{1,0:T(8,128)(2,1)S(1)}, u32[]{:S(2)}, u32[]{:S(2)}) collective-permute-start(bf16[128,128]{1,0:T(8,128)(2,1)S(1)} %get-tuple-element.64), channel_id=1, source_target_pairs={{24,23},{25,18},{26,17},{27,20},{28,19},{29,22},{30,21},{31,16},{1... | collective-permute-start | bytes 98312 | tf_op jit(solution)/shard_map/ppermute | solution.py:249
  37.0 4.5 %collective-permute-start.17 = (bf16[128,128]{1,0:T(8,128)(2,1)S(1)}, bf16[128,128]{1,0:T(8,128)(2,1)S(1)}, u32[]{:S(2)}, u32[]{:S(2)}) collective-permute-start(bf16[128,128]{1,0:T(8,128)(2,1)S(1)} %get-tuple-element.65), channel_id=1, source_target_pairs={{24,17},{25,16},{26,19},{27,18},{28,21},{29,20},{30,23},{31,22},{1... | collective-permute-start | bytes 98312 | tf_op jit(solution)/shard_map/ppermute | solution.py:249
  40.6 3.9 %collective-permute-start.18 = (bf16[128,128]{1,0:T(8,128)(2,1)S(1)}, bf16[128,128]{1,0:T(8,128)(2,1)S(1)}, u32[]{:S(2)}, u32[]{:S(2)}) collective-permute-start(bf16[128,128]{1,0:T(8,128)(2,1)S(1)} %get-tuple-element.66), channel_id=1, source_target_pairs={{24,20},{25,21},{26,22},{27,23},{28,16},{29,17},{30,18},{31,19},{1... | collective-permute-start | bytes 98312 | tf_op jit(solution)/shard_map/ppermute | solution.py:249
  41.0 3.9 %collective-permute-start.19 = (bf16[128,128]{1,0:T(8,128)(2,1)S(1)}, bf16[128,128]{1,0:T(8,128)(2,1)S(1)}, u32[]{:S(2)}, u32[]{:S(2)}) collective-permute-start(bf16[128,128]{1,0:T(8,128)(2,1)S(1)} %get-tuple-element.67), channel_id=1, source_target_pairs={{24,16},{25,17},{26,18},{27,19},{28,20},{29,21},{30,22},{31,23},{1... | collective-permute-start | bytes 98312 | tf_op jit(solution)/shard_map/ppermute | solution.py:249
  45.5 3.5 %collective-permute-start.20 = (bf16[128,128]{1,0:T(8,128)(2,1)S(1)}, bf16[128,128]{1,0:T(8,128)(2,1)S(1)}, u32[]{:S(2)}, u32[]{:S(2)}) collective-permute-start(bf16[128,128]{1,0:T(8,128)(2,1)S(1)} %get-tuple-element.68), channel_id=1, source_target_pairs={{16,15},{17,10},{18,9},{19,12},{20,11},{21,14},{22,13},{23,8},{8,0... | collective-permute-start | bytes 98312 | tf_op jit(solution)/shard_map/ppermute | solution.py:249
  45.6 4.2 %collective-permute-start.21 = (bf16[128,128]{1,0:T(8,128)(2,1)S(1)}, bf16[128,128]{1,0:T(8,128)(2,1)S(1)}, u32[]{:S(2)}, u32[]{:S(2)}) collective-permute-start(bf16[128,128]{1,0:T(8,128)(2,1)S(1)} %get-tuple-element.69), channel_id=1, source_target_pairs={{16,9},{17,8},{18,11},{19,10},{20,13},{21,12},{22,15},{23,14},{8,0... | collective-permute-start | bytes 98312 | tf_op jit(solution)/shard_map/ppermute | solution.py:249
  48.2 2.4 %collective-permute-start.22 = (bf16[128,128]{1,0:T(8,128)(2,1)S(1)}, bf16[128,128]{1,0:T(8,128)(2,1)S(1)}, u32[]{:S(2)}, u32[]{:S(2)}) collective-permute-start(bf16[128,128]{1,0:T(8,128)(2,1)S(1)} %get-tuple-element.70), channel_id=1, source_target_pairs={{16,12},{17,13},{18,14},{19,15},{20,8},{21,9},{22,10},{23,11},{8,0... | collective-permute-start | bytes 98312 | tf_op jit(solution)/shard_map/ppermute | solution.py:249
  49.0 1.9 %collective-permute-start.23 = (bf16[128,128]{1,0:T(8,128)(2,1)S(1)}, bf16[128,128]{1,0:T(8,128)(2,1)S(1)}, u32[]{:S(2)}, u32[]{:S(2)}) collective-permute-start(bf16[128,128]{1,0:T(8,128)(2,1)S(1)} %get-tuple-element.71), channel_id=1, source_target_pairs={{16,8},{17,9},{18,10},{19,11},{20,12},{21,13},{22,14},{23,15},{8,0... | collective-permute-start | bytes 98312 | tf_op jit(solution)/shard_map/ppermute | solution.py:249
  51.5 7.6 %collective-permute-start.24 = (bf16[128,128]{1,0:T(8,128)(2,1)S(1)}, bf16[128,128]{1,0:T(8,128)(2,1)S(1)}, u32[]{:S(2)}, u32[]{:S(2)}) collective-permute-start(bf16[128,128]{1,0:T(8,128)(2,1)S(1)} %get-tuple-element.72), channel_id=1, source_target_pairs={{8,7},{9,2},{10,1},{11,4},{12,3},{13,6},{14,5},{15,0},{0,16},{1,17... | collective-permute-start | bytes 98312 | tf_op jit(solution)/shard_map/ppermute | solution.py:249
  52.6 6.5 %collective-permute-start.25 = (bf16[128,128]{1,0:T(8,128)(2,1)S(1)}, bf16[128,128]{1,0:T(8,128)(2,1)S(1)}, u32[]{:S(2)}, u32[]{:S(2)}) collective-permute-start(bf16[128,128]{1,0:T(8,128)(2,1)S(1)} %get-tuple-element.73), channel_id=1, source_target_pairs={{8,1},{9,0},{10,3},{11,2},{12,5},{13,4},{14,7},{15,6},{0,16},{1,17... | collective-permute-start | bytes 98312 | tf_op jit(solution)/shard_map/ppermute | solution.py:249
  53.8 5.4 %collective-permute-start.26 = (bf16[128,128]{1,0:T(8,128)(2,1)S(1)}, bf16[128,128]{1,0:T(8,128)(2,1)S(1)}, u32[]{:S(2)}, u32[]{:S(2)}) collective-permute-start(bf16[128,128]{1,0:T(8,128)(2,1)S(1)} %get-tuple-element.74), channel_id=1, source_target_pairs={{8,4},{9,5},{10,6},{11,7},{12,0},{13,1},{14,2},{15,3},{0,16},{1,17... | collective-permute-start | bytes 98312 | tf_op jit(solution)/shard_map/ppermute | solution.py:249
  57.2 1.9 %collective-permute-start.27 = (bf16[128,128]{1,0:T(8,128)(2,1)S(1)}, bf16[128,128]{1,0:T(8,128)(2,1)S(1)}, u32[]{:S(2)}, u32[]{:S(2)}) collective-permute-start(bf16[128,128]{1,0:T(8,128)(2,1)S(1)} %get-tuple-element.75), channel_id=1, source_target_pairs={{8,0},{9,1},{10,2},{11,3},{12,4},{13,5},{14,6},{15,7},{0,16},{1,17... | collective-permute-start | bytes 98312 | tf_op jit(solution)/shard_map/ppermute | solution.py:249
  60.5 2.4 %collective-permute-start.28 = (bf16[128,128]{1,0:T(8,128)(2,1)S(1)}, bf16[128,128]{1,0:T(8,128)(2,1)S(1)}, u32[]{:S(2)}, u32[]{:S(2)}) collective-permute-start(bf16[128,128]{1,0:T(8,128)(2,1)S(1)} %get-tuple-element.76), channel_id=1, source_target_pairs={{0,31},{1,26},{2,25},{3,28},{4,27},{5,30},{6,29},{7,24},{24,16},{2... | collective-permute-start | bytes 98312 | tf_op jit(solution)/shard_map/ppermute | solution.py:249
  61.3 1.6 %collective-permute-start.29 = (bf16[128,128]{1,0:T(8,128)(2,1)S(1)}, bf16[128,128]{1,0:T(8,128)(2,1)S(1)}, u32[]{:S(2)}, u32[]{:S(2)}) collective-permute-start(bf16[128,128]{1,0:T(8,128)(2,1)S(1)} %get-tuple-element.77), channel_id=1, source_target_pairs={{0,25},{1,24},{2,27},{3,26},{4,29},{5,28},{6,31},{7,30},{24,16},{2... | collective-permute-start | bytes 98312 | tf_op jit(solution)/shard_map/ppermute | solution.py:249
  61.3 2.1 %collective-permute-start.30 = (bf16[128,128]{1,0:T(8,128)(2,1)S(1)}, bf16[128,128]{1,0:T(8,128)(2,1)S(1)}, u32[]{:S(2)}, u32[]{:S(2)}) collective-permute-start(bf16[128,128]{1,0:T(8,128)(2,1)S(1)} %get-tuple-element.78), channel_id=1, source_target_pairs={{0,28},{1,29},{2,30},{3,31},{4,24},{5,25},{6,26},{7,27},{24,16},{2... | collective-permute-start | bytes 98312 | tf_op jit(solution)/shard_map/ppermute | solution.py:249
  61.8 2.6 %collective-permute-start.31 = (bf16[128,128]{1,0:T(8,128)(2,1)S(1)}, bf16[128,128]{1,0:T(8,128)(2,1)S(1)}, u32[]{:S(2)}, u32[]{:S(2)}) collective-permute-start(bf16[128,128]{1,0:T(8,128)(2,1)S(1)} %get-tuple-element.79), channel_id=1, source_target_pairs={{0,24},{1,25},{2,26},{3,27},{4,28},{5,29},{6,30},{7,31},{24,16},{2... | collective-permute-start | bytes 98312 | tf_op jit(solution)/shard_map/ppermute | solution.py:249
  65.1 5.4 %collective-permute-start.32 = (f32[1,6,16,128]{3,2,1,0:T(8,128)S(1)}, f32[1,6,16,128]{3,2,1,0:T(8,128)S(1)}, u32[]{:S(2)}, u32[]{:S(2)}) collective-permute-start(f32[1,6,16,128]{3,2,1,0:T(8,128)S(1)} %shard_map.72), channel_id=1, source_target_pairs={{0,8},{8,16},{16,24},{24,0},{1,9},{9,17},{17,25},{25,1},{2,10},{10... | collective-permute-start | bytes 147464 | tf_op jit(solution)/shard_map/ppermute | solution.py:261

commit v3 on v0

v3 whole, which is shorter than its diff:
```python
import functools

import jax
import jax.numpy as jnp
from jax import lax
from jax.experimental import pallas as pl
from jax.experimental.pallas import tpu as pltpu
from jax.sharding import PartitionSpec as P

SUB = 8
GROUP = 64
NT = (((1,), (1,)), ((), ()))
VMEM = pl.BlockSpec(memory_space=pltpu.VMEM)
SMEM = pl.BlockSpec(memory_space=pltpu.SMEM)
HBM = pl.BlockSpec(memory_space=pltpu.HBM)
DMA = pltpu.SemaphoreType.DMA


def modulo(value, divisor):
    if divisor & (divisor - 1) == 0:
        return value & (divisor - 1)
    return lax.rem(value, divisor)


def rows_of(ref, index):
    return ref.at[pl.ds(pl.multiple_of(index * SUB, SUB), SUB)]


def products(start, stop, group, table, tiles, x, acc):
    block = tiles.shape[-1]

    def round_of(g, carry):
        first = start + g * group
        terms = []
        for u in range(0, group, 2):
            s = first + u
            pair = jnp.concatenate([rows_of(x, table[1, s])[...], rows_of(x, table[1, s + 1])[...]], axis=0)
            both = tiles[pl.ds(s, 2)].reshape(2 * block, block)
            terms.append(
                lax.dot_general(pair.astype(jnp.bfloat16), both, NT, preferred_element_type=jnp.float32)
            )
        for u in range(0, group, 2):
            s = first + u
            term = terms[u // 2]
            rows_of(acc, table[0, s])[...] += term[:SUB, :block]
            rows_of(acc, table[0, s + 1])[...] += term[SUB:, block:]
        return carry

    lax.fori_loop(0, (stop - start + group - 1) // group, round_of, 0)


def places(acc, own):
    nblk = acc.shape[0] // SUB - 1
    odd = lax.rem(lax.axis_index("cols"), 2) == 1
    return jnp.where(odd, own, nblk - own), nblk // 2, jnp.where(odd, nblk - own, own), 0


def clear(acc, own):
    for at in places(acc, own):
        acc[pl.ds(at * SUB, own * SUB)] = jnp.zeros((own * SUB, acc.shape[1]), acc.dtype)


def write_terms(acc, outs, own):
    for at, out in zip(places(acc, own), outs):
        for t in range(out.shape[0] // own):
            rows = acc[pl.ds(at * SUB + t, own, stride=SUB)]
            out[pl.ds(t * own, own)] = rows.astype(out.dtype)


def arrived_state(wet, arrived):
    total = arrived[0][...].astype(jnp.float32)
    for ref in arrived[1:]:
        total += ref[...].astype(jnp.float32)
    return total.reshape(-1, *wet.shape) * wet[...]


def set_x(x, values):
    x[...] = jnp.zeros_like(x)
    own = values.shape[1]
    for t in range(values.shape[0]):
        x[pl.ds(t, own, stride=SUB)] = values[t]


def taking(step, parts, tiles, kept, sems):
    size = kept.shape[0] // parts

    def load(i):
        part = pl.ds(i * size, size)
        return pltpu.make_async_copy(tiles.at[0, part], kept.at[part], sems.at[i])

    return size, load


def stream(step, parts, live, size, load, table, kept, x, acc):
    for i in range(parts):
        if i >= step:
            load(i).wait()

        @pl.when(live > i * size)
        def _():
            stop = jnp.minimum(live, (i + 1) * size)
            products(i * size, stop, min(size, GROUP), table, kept, x, acc)


def first_kernel(
    months, ncols, count, rows, cols, depth, forcing, tiles,
    o0, o1, o2, o3, kept, table, wet, force,
    x, acc, entries, rows_in, cols_in, depth_in, sems, own_sems,
):
    own, width = depth.shape
    block = forcing.shape[-1]
    nblk = own * ncols
    parts = months
    size, load = taking(0, parts, tiles, kept, sems)
    active = lax.axis_index("month") == months - 1

    small = [
        pltpu.make_async_copy(source, target, own_sems.at[i])
        for i, (source, target) in enumerate(
            [(rows, rows_in), (cols, cols_in), (depth, depth_in), (forcing, force)]
        )
    ]
    for copy in small:
        copy.start()
    load(0).start()

    @pl.when(active)
    def _():
        for i in range(1, parts):
            load(i).start()

    live = count[0, 0]
    base = nblk - lax.axis_index("cols") * own
    small[0].wait()
    small[1].wait()
    slot = lax.broadcasted_iota(jnp.int32, rows.shape, 1)
    entries[0:1, :] = jnp.where(slot < live, modulo(rows_in[...] + base, nblk), nblk)
    entries[1:2, :] = modulo(cols_in[...], own)
    entries[2:3, :] = jnp.full(rows.shape, live, jnp.int32)
    listing = pltpu.make_async_copy(entries, table, own_sems.at[4])
    listing.start()

    small[2].wait()
    small[3].wait()
    lane = lax.broadcasted_iota(jnp.int32, (width, block), 1)
    column = lax.broadcasted_iota(jnp.int32, (width, block), 0)
    spread = (lax.rem(lane, width) == column).astype(jnp.float32)
    below = jnp.dot(depth_in[...].astype(jnp.float32), spread, preferred_element_type=jnp.float32)
    level = lax.div(lax.broadcasted_iota(jnp.int32, (own, block), 1), width).astype(jnp.float32)
    wet[...] = (level < below).astype(jnp.float32)

    @pl.when(active)
    def _():
        set_x(x, force[0])
        clear(acc, own)

    listing.wait()

    @pl.when(active)
    def _():
        stream(0, parts, live, size, load, table, kept, x, acc)
        write_terms(acc, (o0, o1, o2, o3), own)

    @pl.when(jnp.logical_not(active))
    def _():
        load(0).wait()


def taking_kernel(
    step, months, table, wet, force, r0, r1, r2, r3, kept_in, tiles,
    o0, o1, o2, o3, kept, x, acc, sems,
):
    own = wet.shape[0]
    parts = months
    month = months - 1 - step
    size, load = taking(step, parts, tiles, kept, sems)
    my_month = lax.axis_index("month")

    @pl.when(my_month <= month)
    def _():
        load(step).start()

    @pl.when(my_month < month)
    def _():
        load(step).wait()

    @pl.when(my_month == month)
    def _():
        for i in range(step + 1, parts):
            load(i).start()
        set_x(x, arrived_state(wet, (r0, r1, r2, r3)) + force[0])
        clear(acc, own)
        stream(step, parts, table[2, 0], size, load, table, kept, x, acc)
        write_terms(acc, (o0, o1, o2, o3), own)


def step_kernel(
    month, table, wet, force, r0, r1, r2, r3, tiles,
    o0, o1, o2, o3, state, x, acc,
):
    own = wet.shape[0]

    @pl.when(lax.axis_index("month") == month)
    def _():
        arrived = arrived_state(wet, (r0, r1, r2, r3))
        state[0] = arrived
        set_x(x, arrived + force[0])
        clear(acc, own)
        products(0, table[2, 0], GROUP, table, tiles, x, acc)
        write_terms(acc, (o0, o1, o2, o3), own)


def held_kernel(*refs):
    states, out = refs[:-1], refs[-1]
    for m, state in enumerate(states):

        @pl.when(lax.axis_index("month") == m)
        def _():
            out[...] = state[...]


def last_kernel(wet, r0, r1, r2, r3, out):
    out[0] = arrived_state(wet, (r0, r1, r2, r3))


def in_hbm(value):
    return pltpu.with_memory_space_constraint(value, pltpu.HBM)


def call(kernel, operands, in_specs, outs, out_specs, scratch=(), aliases={}):
    return pl.pallas_call(
        kernel,
        out_shape=outs,
        in_specs=in_specs,
        out_specs=out_specs,
        scratch_shapes=list(scratch),
        input_output_aliases=aliases,
        compiler_params=pltpu.CompilerParams(vmem_limit_bytes=12 * 2**20),
    )(*operands)


def hops(k, active, target, months, ncols, move):
    if months != 4:
        ring = [target] + [m for m in range(months) if m not in (active, target)] + [active]
        then = dict(zip(ring, ring[1:]))
    elif active ^ 1 == target:
        mine, yours = active ^ 2, target ^ 2
        if k < 2:
            then = {target: yours, yours: mine, mine: active}
        else:
            then = {target: active, yours: mine, mine: yours}
    else:
        mine, yours = active ^ 1, target ^ 1
        then = {target: yours, yours: mine, mine: active}
    pairs = [(active * ncols + c, target * ncols + move(c)) for c in range(ncols)]
    for source, to in then.items():
        pairs += [(source * ncols + c, to * ncols + c) for c in range(ncols)]
    return pairs


def on_device(forcing, tiles, tile_rows, tile_cols, tile_count, depth):
    months = lax.axis_size("month")
    ncols = lax.axis_size("cols")
    own, tracers, block = forcing.shape[1:]
    slots = tiles.shape[1]
    nblk = own * ncols
    far = lambda c: (c + 1) % ncols if c % 2 else (c - 1) % ncols
    near = lambda c: c ^ 1
    opposite = lambda c: (c + ncols // 2) % ncols
    moves = [far, opposite, near, lambda c: c]

    term = jax.ShapeDtypeStruct((tracers * own, block), jnp.bfloat16)
    plane = jax.ShapeDtypeStruct((1, tracers, own, block), jnp.float32)
    mask = jax.ShapeDtypeStruct((own, block), jnp.float32)
    kept_like = pltpu.VMEM((slots, block, block), tiles.dtype)
    scratch = [
        pltpu.VMEM((own * SUB, block), jnp.float32),
        pltpu.VMEM(((nblk + 1) * SUB, block), jnp.float32),
    ]
    tiles = in_hbm(tiles)
    forcing = forcing.transpose(0, 2, 1, 3)
    *terms, kept, table, wet, force = call(
        functools.partial(first_kernel, months, ncols),
        (tile_count, in_hbm(tile_rows), in_hbm(tile_cols), in_hbm(depth), in_hbm(forcing), tiles),
        [SMEM] + [HBM] * 5,
        [term] * 4 + [kept_like, pltpu.SMEM((3, slots), jnp.int32), mask, plane],
        [VMEM] * 5 + [SMEM, VMEM, VMEM],
        scratch
        + [
            pltpu.VMEM((3, slots), jnp.int32),
            pltpu.VMEM(tile_rows.shape, jnp.int32),
            pltpu.VMEM(tile_cols.shape, jnp.int32),
            pltpu.VMEM(depth.shape, jnp.int32),
            DMA((months,)),
            DMA((5,)),
        ],
    )
    states = []
    for step in range(2 * months):
        month = months - 1 - step % months
        if 0 < step < months:
            *terms, kept = call(
                functools.partial(taking_kernel, step, months),
                (table, wet, force, *arrived, kept, tiles),
                [SMEM] + [VMEM] * 7 + [HBM],
                [term] * 4 + [kept_like],
                [VMEM] * 5,
                scratch + [DMA((months,))],
                {7: 4},
            )
        elif step > 0:
            *terms, state = call(
                functools.partial(step_kernel, month),
                (table, wet, force, *arrived, kept),
                [SMEM] + [VMEM] * 7,
                [term] * 4 + [plane],
                [VMEM] * 5,
                scratch,
            )
            states.insert(0, state)
        target = month - 1 if month else months - 1 if step < months else 1
        arrived = [
            lax.ppermute(term, ("month", "cols"), hops(k, month, target, months, ncols, move))
            for k, (term, move) in enumerate(zip(terms, moves))
        ]

    (held,) = call(held_kernel, states, [VMEM] * months, [plane], [VMEM])
    passed = lax.ppermute(held, "month", [(m, (m + 1) % months) for m in range(months)])
    (last,) = call(last_kernel, (wet, *arrived), [VMEM] * 5, [plane], [VMEM])
    crossed = lax.ppermute(last, "month", [(m, m ^ 1) for m in range(months)])
    result = jnp.where(lax.axis_index("month") == 0, crossed, passed)
    return result.transpose(0, 2, 1, 3)


def solution(mesh):
    in_specs = (
        P("month", "cols", None, None),
        P("month", "cols", None, None),
        P("month", "cols"),
        P("month", "cols"),
        P("month", "cols"),
        P("cols", None),
    )
    out_specs = P("month", "cols", None, None)
    return jax.shard_map(
        on_device, mesh=mesh, in_specs=in_specs, out_specs=out_specs, check_vma=False
    )
```

time: 826 us -> 60.7 us (0.07)
  waiting for transfers between devices: 708 us -> 22.2 us
  other arithmetic: 75.4 us -> 0.63 us
  starting transfers between devices: 0.79 us -> 27.5 us
  matrix products: 13.4 us -> 0 us
  between operations: 13.4 us -> 0.81 us
  local copies, waits for them, and re-layouts: 10.4 us -> 0 us
  Pallas kernels: 0 us -> 8.37 us
    reduce_scatter x8 -> x0, waiting for transfers between devices: 695 us -> none  [reduce_terms(): lax.psum_scatter(partial_terms.astype(jnp.bfloat16), 'cols', scatter_dime...]
    scatter-add x2 -> x0, other arithmetic: 50.8 us -> none  [place(): buffer.at[target].add(terms * inside.astype(jnp.float32)[:, None, None])]
    ppermute x8 -> x34, starting transfers between devices: 0.46 us -> 27.5 us  [the longest x32 27.3 us: on_device(): lax.ppermute(term, ('month', 'cols'), hops(k, month, target, months, ncol...]
    convert_element_type x26 -> x0, other arithmetic: 15.5 us -> none  [the longest x8 14.1 us: reduce_terms(): partial_terms.astype(jnp.bfloat16)]
    dot_general x2 -> x0, matrix products: 13.4 us -> none  [compute(): jnp.einsum('stj,sij->sti', picked, plates, preferred_element_type=jnp.flo...]
    ppermute x8 -> x34, waiting for transfers between devices: 12.7 us -> 22.2 us  [the longest x32 21 us: on_device(): lax.ppermute(term, ('month', 'cols'), hops(k, month, target, months, ncol...]
    pallas_call x0 -> x10, Pallas kernels: none -> 8.37 us  [call(): pl.pallas_call(kernel, out_shape=outs, in_specs=in_specs, out_specs=out_s...]
  transfers between devices with their start and end apart: 16 -> 34, of which waited for: 16 -> 19; matrix products, arithmetic and copies ran while one was open for 0% -> 0% of each run, Pallas kernels for 0% -> 0%
where the time goes in v3:
time: 60.7 us; the launch traced here: 59.5 us
  starting transfers between devices  27.5 us (45%)
  waiting for transfers between devices  22.2 us (37%)
  Pallas kernels  8.37 us (14%)
  between operations  0.81 us (1%)
  other arithmetic  0.63 us (1%)
    ppermute x32, starting transfers between devices, on_device(): lax.ppermute(term, ('month', 'cols'), hops(k, month, target, months, ncol...  27.3 us
    ppermute x32, waiting for transfers between devices, on_device(): lax.ppermute(term, ('month', 'cols'), hops(k, month, target, months, ncol...  21 us
    pallas_call x10, Pallas kernels, call(): pl.pallas_call(kernel, out_shape=outs, in_specs=in_specs, out_specs=out_s...  8.37 us
  transfers between devices with their start and end apart: 34, of which 19 were waited for; matrix products, arithmetic and copies ran while one was open for 0% of the time, Pallas kernels for 0%

profile of v3, /device:TPU:0, one launch (start us, length us, event | category | flops | bytes accessed | tf_op | source)
XLA Modules:
  0.0 59.5 jit_solution(7230396693694322811)
XLA Ops:
  0.7 2.0 %shard_map.64 = (bf16[96,128]{1,0:T(8,128)(2,1)S(1)}, bf16[96,128]{1,0:T(8,128)(2,1)S(1)}, bf16[96,128]{1,0:T(8,128)(2,1)S(1)}, bf16[96,128]{1,0:T(8,128)(2,1)S(...) custom-call(s32[1,1]{1,0:T(1,128)S(6)} %copy.13.count, ...), custom_call_target="tpu_custom_call" | custom-call | tf_op jit(solution)/shard_map/pallas_call | solution.py:231
  2.7 0.5 collective-permute-start
  3.2 3.7 %collective-permute-start.1 = (bf16[96,128]{1,0:T(8,128)(2,1)S(1)}, bf16[96,128]{1,0:T(8,128)(2,1)S(1)}, u32[]{:S(2)}, u32[]{:S(2)}) collective-permute-start(bf16[96,128]{1,0:T(8,128)(2,1)S(1)} %get-tuple-element.52), channel_id=1, source_target_pairs={{24,20},{25,21},{26,22},{27,23},{28,16},{29,17},{30,18},{31,19},{1... | collective-permute-start | bytes 73736 | tf_op jit(solution)/shard_map/ppermute | solution.py:323
  6.9 3.2 %collective-permute-start.2 = (bf16[96,128]{1,0:T(8,128)(2,1)S(1)}, bf16[96,128]{1,0:T(8,128)(2,1)S(1)}, u32[]{:S(2)}, u32[]{:S(2)}) collective-permute-start(bf16[96,128]{1,0:T(8,128)(2,1)S(1)} %get-tuple-element.53), channel_id=1, source_target_pairs={{24,17},{25,16},{26,19},{27,18},{28,21},{29,20},{30,23},{31,22},{1... | collective-permute-start | bytes 73736 | tf_op jit(solution)/shard_map/ppermute | solution.py:323
  10.1 0.8 %collective-permute-done.2.r2 = bf16[96,128]{1,0:T(8,128)(2,1)S(1)} collective-permute-done((bf16[96,128]{1,0:T(8,128)(2,1)S(1)}, bf16[96,128]{1,0:T(8,128)(2,1)S(1)}, u32[]{:S(2)}, u32[]{:S(2)}) %collective-permute-start.2) | collective-permute-done | bytes 24608 | tf_op jit(solution)/shard_map/ppermute | solution.py:323
  10.9 0.3 collective-permute-done.3.r3
  11.3 1.6 %shard_map.65 = (bf16[96,128]{1,0:T(8,128)(2,1)S(1)}, bf16[96,128]{1,0:T(8,128)(2,1)S(1)}, bf16[96,128]{1,0:T(8,128)(2,1)S(1)}, bf16[96,128]{1,0:T(8,128)(2,1)S(1)}, bf16[256,128,128]{2,1,0:T(8,128)(2,1)S(1)}) custom-call(s32[3,256]{1,0:T(4,128)S(4)} %get-tuple-element.49.table, ...), custom_call_target="tpu_custom_call", output_to_operand_aliasing={{4}: (7, {})} | custom-call | tf_op jit(solution)/shard_map/pallas_call | solution.py:231
  13.0 3.0 %collective-permute-start.5 = (bf16[96,128]{1,0:T(8,128)(2,1)S(1)}, bf16[96,128]{1,0:T(8,128)(2,1)S(1)}, u32[]{:S(2)}, u32[]{:S(2)}) collective-permute-start(bf16[96,128]{1,0:T(8,128)(2,1)S(1)} %get-tuple-element.57), channel_id=1, source_target_pairs={{16,12},{17,13},{18,14},{19,15},{20,8},{21,9},{22,10},{23,11},{8,0... | collective-permute-start | bytes 73736 | tf_op jit(solution)/shard_map/ppermute | solution.py:323
  16.1 1.4 %collective-permute-done.5.r1 = bf16[96,128]{1,0:T(8,128)(2,1)S(1)} collective-permute-done((bf16[96,128]{1,0:T(8,128)(2,1)S(1)}, bf16[96,128]{1,0:T(8,128)(2,1)S(1)}, u32[]{:S(2)}, u32[]{:S(2)}) %collective-permute-start.5) | collective-permute-done | bytes 24608 | tf_op jit(solution)/shard_map/ppermute | solution.py:323
  17.5 0.2 collective-permute-done.6.r2
  17.7 0.2 collective-permute-done.7.r3
  17.9 1.6 %shard_map.66 = (bf16[96,128]{1,0:T(8,128)(2,1)S(1)}, bf16[96,128]{1,0:T(8,128)(2,1)S(1)}, bf16[96,128]{1,0:T(8,128)(2,1)S(1)}, bf16[96,128]{1,0:T(8,128)(2,1)S(1)}, bf16[256,128,128]{2,1,0:T(8,128)(2,1)S(1)}) custom-call(s32[3,256]{1,0:T(4,128)S(4)} %get-tuple-element.49.table, ...), custom_call_target="tpu_custom_call", output_to_operand_aliasing={{4}: (7, {})} | custom-call | tf_op jit(solution)/shard_map/pallas_call | solution.py:231
  19.6 3.1 %collective-permute-start.10 = (bf16[96,128]{1,0:T(8,128)(2,1)S(1)}, bf16[96,128]{1,0:T(8,128)(2,1)S(1)}, u32[]{:S(2)}, u32[]{:S(2)}) collective-permute-start(bf16[96,128]{1,0:T(8,128)(2,1)S(1)} %get-tuple-element.63), channel_id=1, source_target_pairs={{8,1},{9,0},{10,3},{11,2},{12,5},{13,4},{14,7},{15,6},{0,8},{1,9},... | collective-permute-start | bytes 73736 | tf_op jit(solution)/shard_map/ppermute | solution.py:323
  22.6 0.1 collective-permute-start.11
  22.7 1.1 %collective-permute-done.10.r2 = bf16[96,128]{1,0:T(8,128)(2,1)S(1)} collective-permute-done((bf16[96,128]{1,0:T(8,128)(2,1)S(1)}, bf16[96,128]{1,0:T(8,128)(2,1)S(1)}, u32[]{:S(2)}, u32[]{:S(2)}) %collective-permute-start.10) | collective-permute-done | bytes 24608 | tf_op jit(solution)/shard_map/ppermute | solution.py:323
  23.8 4.8 %collective-permute-done.8.r0 = bf16[96,128]{1,0:T(8,128)(2,1)S(1)} collective-permute-done((bf16[96,128]{1,0:T(8,128)(2,1)S(1)}, bf16[96,128]{1,0:T(8,128)(2,1)S(1)}, u32[]{:S(2)}, u32[]{:S(2)}) %collective-permute-start.8) | collective-permute-done | bytes 24608 | tf_op jit(solution)/shard_map/ppermute | solution.py:323
  28.7 1.7 %shard_map.67 = (bf16[96,128]{1,0:T(8,128)(2,1)S(1)}, bf16[96,128]{1,0:T(8,128)(2,1)S(1)}, bf16[96,128]{1,0:T(8,128)(2,1)S(1)}, bf16[96,128]{1,0:T(8,128)(2,1)S(1)}, bf16[256,128,128]{2,1,0:T(8,128)(2,1)S(1)}) custom-call(s32[3,256]{1,0:T(4,128)S(4)} %get-tuple-element.49.table, ...), custom_call_target="tpu_custom_call", output_to_operand_aliasing={{4}: (7, {})} | custom-call | tf_op jit(solution)/shard_map/pallas_call | solution.py:231
  30.5 2.1 %collective-permute-start.15 = (bf16[96,128]{1,0:T(8,128)(2,1)S(1)}, bf16[96,128]{1,0:T(8,128)(2,1)S(1)}, u32[]{:S(2)}, u32[]{:S(2)}) collective-permute-start(bf16[96,128]{1,0:T(8,128)(2,1)S(1)} %get-tuple-element.69), channel_id=1, source_target_pairs={{0,24},{1,25},{2,26},{3,27},{4,28},{5,29},{6,30},{7,31},{24,16},{2... | collective-permute-start | bytes 73736 | tf_op jit(solution)/shard_map/ppermute | solution.py:323
  32.7 1.6 %collective-permute-done.15.r3 = bf16[96,128]{1,0:T(8,128)(2,1)S(1)} collective-permute-done((bf16[96,128]{1,0:T(8,128)(2,1)S(1)}, bf16[96,128]{1,0:T(8,128)(2,1)S(1)}, u32[]{:S(2)}, u32[]{:S(2)}) %collective-permute-start.15) | collective-permute-done | bytes 24608 | tf_op jit(solution)/shard_map/ppermute | solution.py:323
  34.3 0.4 collective-permute-start.16
  34.7 2.4 %collective-permute-start.17 = (bf16[96,128]{1,0:T(8,128)(2,1)S(1)}, bf16[96,128]{1,0:T(8,128)(2,1)S(1)}, u32[]{:S(2)}, u32[]{:S(2)}) collective-permute-start(bf16[96,128]{1,0:T(8,128)(2,1)S(1)} %get-tuple-element.72), channel_id=1, source_target_pairs={{24,20},{25,21},{26,22},{27,23},{28,16},{29,17},{30,18},{31,19},{1... | collective-permute-start | bytes 73736 | tf_op jit(solution)/shard_map/ppermute | solution.py:323
  37.1 0.1 collective-permute-start.18
  37.2 0.4 collective-permute-start.19
  37.6 0.5 collective-permute-done.16.r0
  38.1 0.4 collective-permute-done.17.r1
  38.5 1.8 %collective-permute-start.20 = (bf16[96,128]{1,0:T(8,128)(2,1)S(1)}, bf16[96,128]{1,0:T(8,128)(2,1)S(1)}, u32[]{:S(2)}, u32[]{:S(2)}) collective-permute-start(bf16[96,128]{1,0:T(8,128)(2,1)S(1)} %get-tuple-element.75), channel_id=1, source_target_pairs={{16,15},{17,10},{18,9},{19,12},{20,11},{21,14},{22,13},{23,8},{8,0... | collective-permute-start | bytes 73736 | tf_op jit(solution)/shard_map/ppermute | solution.py:323
  40.3 2.6 %collective-permute-start.21 = (bf16[96,128]{1,0:T(8,128)(2,1)S(1)}, bf16[96,128]{1,0:T(8,128)(2,1)S(1)}, u32[]{:S(2)}, u32[]{:S(2)}) collective-permute-start(bf16[96,128]{1,0:T(8,128)(2,1)S(1)} %get-tuple-element.76), channel_id=1, source_target_pairs={{16,12},{17,13},{18,14},{19,15},{20,8},{21,9},{22,10},{23,11},{8,0... | collective-permute-start | bytes 73736 | tf_op jit(solution)/shard_map/ppermute | solution.py:323
  42.9 0.1 collective-permute-start.22
  43.0 1.4 %collective-permute-done.21.r1 = bf16[96,128]{1,0:T(8,128)(2,1)S(1)} collective-permute-done((bf16[96,128]{1,0:T(8,128)(2,1)S(1)}, bf16[96,128]{1,0:T(8,128)(2,1)S(1)}, u32[]{:S(2)}, u32[]{:S(2)}) %collective-permute-start.21) | collective-permute-done | bytes 24608 | tf_op jit(solution)/shard_map/ppermute | solution.py:323
  44.4 0.2 collective-permute-done.22.r2
  44.6 0.2 collective-permute-done.23.r3
  44.9 1.7 %collective-permute-start.24 = (bf16[96,128]{1,0:T(8,128)(2,1)S(1)}, bf16[96,128]{1,0:T(8,128)(2,1)S(1)}, u32[]{:S(2)}, u32[]{:S(2)}) collective-permute-start(bf16[96,128]{1,0:T(8,128)(2,1)S(1)} %get-tuple-element.79), channel_id=1, source_target_pairs={{8,7},{9,2},{10,1},{11,4},{12,3},{13,6},{14,5},{15,0},{0,16},{1,17... | collective-permute-start | bytes 73736 | tf_op jit(solution)/shard_map/ppermute | solution.py:323
  46.5 0.5 collective-permute-start.25
  47.1 0.5 collective-permute-start.26
  47.6 0.1 collective-permute-start.27
  47.7 3.1 %collective-permute-done.24.r0 = bf16[96,128]{1,0:T(8,128)(2,1)S(1)} collective-permute-done((bf16[96,128]{1,0:T(8,128)(2,1)S(1)}, bf16[96,128]{1,0:T(8,128)(2,1)S(1)}, u32[]{:S(2)}, u32[]{:S(2)}) %collective-permute-start.24) | collective-permute-done | bytes 24608 | tf_op jit(solution)/shard_map/ppermute | solution.py:323
  50.8 0.9 %collective-permute-done.25.r1 = bf16[96,128]{1,0:T(8,128)(2,1)S(1)} collective-permute-done((bf16[96,128]{1,0:T(8,128)(2,1)S(1)}, bf16[96,128]{1,0:T(8,128)(2,1)S(1)}, u32[]{:S(2)}, u32[]{:S(2)}) %collective-permute-start.25) | collective-permute-done | bytes 24608 | tf_op jit(solution)/shard_map/ppermute | solution.py:323
  51.8 1.4 %shard_map.71 = (bf16[96,128]{1,0:T(8,128)(2,1)S(1)}, bf16[96,128]{1,0:T(8,128)(2,1)S(1)}, bf16[96,128]{1,0:T(8,128)(2,1)S(1)}, bf16[96,128]{1,0:T(8,128)(2,1)S(1)}, f32[1,6,16,128]{3,2,1,0:T(8,128)S(1)}) custom-call(s32[3,256]{1,0:T(4,128)S(4)} %get-tuple-element.49.table, f32[16,128]{1,0:T(8,128)S(1)} %get-tuple-element.48.wet, ...), custom_call_target="tpu_custom_call" | custom-call | tf_op jit(solution)/shard_map/pallas_call | solution.py:231
  53.2 0.1 collective-permute-start.28
  53.2 0.1 collective-permute-start.29
  53.4 0.5 collective-permute-start.31
  53.9 0.1 collective-permute-start.33
  54.0 3.1 %collective-permute-done.28.r0 = bf16[96,128]{1,0:T(8,128)(2,1)S(1)} collective-permute-done((bf16[96,128]{1,0:T(8,128)(2,1)S(1)}, bf16[96,128]{1,0:T(8,128)(2,1)S(1)}, u32[]{:S(2)}, u32[]{:S(2)}) %collective-permute-start.28) | collective-permute-done | bytes 24608 | tf_op jit(solution)/shard_map/ppermute | solution.py:323
  57.1 0.4 collective-permute-done.29.r1
  57.5 0.1 collective-permute-start.32
  57.6 0.2 collective-permute-done.33
  57.9 1.0 %collective-permute-done.32 = f32[1,6,16,128]{3,2,1,0:T(8,128)S(1)} collective-permute-done((f32[1,6,16,128]{3,2,1,0:T(8,128)S(1)}, f32[1,6,16,128]{3,2,1,0:T(8,128)S(1)}, u32[]{:S(2)}, u32[]{:S(2)}) %collective-permute-start.32) | collective-permute-done | bytes 49184 | tf_op jit(solution)/shard_map/ppermute | solution.py:330
  58.8 0.6 %select_bitcast_fusion = f32[1,16,6,128]{3,1,2,0:T(8,128)} fusion(f32[1,6,16,128]{3,2,1,0:T(8,128)S(1)} %collective-permute-done.32, f32[1,6,16,128]{3,2,1,0:T(8,128)S(1)} %collective-permute-done.33, pred[]{:T(512)S(6)} %eq.3), kind=kLoop, calls=%fused_computation | loop fusion | flops 12288 | bytes 147457 | tf_op jit(solution)/shard_map/transpose | solution.py:332
  (31 shorter events, 0.6 us)
Async XLA Ops:
  2.7 7.4 %collective-permute-start = (bf16[96,128]{1,0:T(8,128)(2,1)S(1)}, bf16[96,128]{1,0:T(8,128)(2,1)S(1)}, u32[]{:S(2)}, u32[]{:S(2)}) collective-permute-start(bf16[96,128]{1,0:T(8,128)(2,1)S(1)} %get-tuple-element.51), channel_id=1, source_target_pairs={{24,23},{25,18},{26,17},{27,20},{28,19},{29,22},{30,21},{31,16},{1... | collective-permute-start | bytes 73736 | tf_op jit(solution)/shard_map/ppermute | solution.py:323
  3.2 6.9 %collective-permute-start.1 = (bf16[96,128]{1,0:T(8,128)(2,1)S(1)}, bf16[96,128]{1,0:T(8,128)(2,1)S(1)}, u32[]{:S(2)}, u32[]{:S(2)}) collective-permute-start(bf16[96,128]{1,0:T(8,128)(2,1)S(1)} %get-tuple-element.52), channel_id=1, source_target_pairs={{24,20},{25,21},{26,22},{27,23},{28,16},{29,17},{30,18},{31,19},{1... | collective-permute-start | bytes 73736 | tf_op jit(solution)/shard_map/ppermute | solution.py:323
  6.9 4.0 %collective-permute-start.2 = (bf16[96,128]{1,0:T(8,128)(2,1)S(1)}, bf16[96,128]{1,0:T(8,128)(2,1)S(1)}, u32[]{:S(2)}, u32[]{:S(2)}) collective-permute-start(bf16[96,128]{1,0:T(8,128)(2,1)S(1)} %get-tuple-element.53), channel_id=1, source_target_pairs={{24,17},{25,16},{26,19},{27,18},{28,21},{29,20},{30,23},{31,22},{1... | collective-permute-start | bytes 73736 | tf_op jit(solution)/shard_map/ppermute | solution.py:323
  10.1 1.2 %collective-permute-start.3 = (bf16[96,128]{1,0:T(8,128)(2,1)S(1)}, bf16[96,128]{1,0:T(8,128)(2,1)S(1)}, u32[]{:S(2)}, u32[]{:S(2)}) collective-permute-start(bf16[96,128]{1,0:T(8,128)(2,1)S(1)} %get-tuple-element.54), channel_id=1, source_target_pairs={{24,16},{25,17},{26,18},{27,19},{28,20},{29,21},{30,22},{31,23},{1... | collective-permute-start | bytes 73736 | tf_op jit(solution)/shard_map/ppermute | solution.py:323
  12.9 3.2 %collective-permute-start.4 = (bf16[96,128]{1,0:T(8,128)(2,1)S(1)}, bf16[96,128]{1,0:T(8,128)(2,1)S(1)}, u32[]{:S(2)}, u32[]{:S(2)}) collective-permute-start(bf16[96,128]{1,0:T(8,128)(2,1)S(1)} %get-tuple-element.56), channel_id=1, source_target_pairs={{16,15},{17,10},{18,9},{19,12},{20,11},{21,14},{22,13},{23,8},{8,0... | collective-permute-start | bytes 73736 | tf_op jit(solution)/shard_map/ppermute | solution.py:323
  13.0 4.5 %collective-permute-start.5 = (bf16[96,128]{1,0:T(8,128)(2,1)S(1)}, bf16[96,128]{1,0:T(8,128)(2,1)S(1)}, u32[]{:S(2)}, u32[]{:S(2)}) collective-permute-start(bf16[96,128]{1,0:T(8,128)(2,1)S(1)} %get-tuple-element.57), channel_id=1, source_target_pairs={{16,12},{17,13},{18,14},{19,15},{20,8},{21,9},{22,10},{23,11},{8,0... | collective-permute-start | bytes 73736 | tf_op jit(solution)/shard_map/ppermute | solution.py:323
  15.9 1.8 %collective-permute-start.6 = (bf16[96,128]{1,0:T(8,128)(2,1)S(1)}, bf16[96,128]{1,0:T(8,128)(2,1)S(1)}, u32[]{:S(2)}, u32[]{:S(2)}) collective-permute-start(bf16[96,128]{1,0:T(8,128)(2,1)S(1)} %get-tuple-element.58), channel_id=1, source_target_pairs={{16,9},{17,8},{18,11},{19,10},{20,13},{21,12},{22,15},{23,14},{8,0... | collective-permute-start | bytes 73736 | tf_op jit(solution)/shard_map/ppermute | solution.py:323
  16.0 1.9 %collective-permute-start.7 = (bf16[96,128]{1,0:T(8,128)(2,1)S(1)}, bf16[96,128]{1,0:T(8,128)(2,1)S(1)}, u32[]{:S(2)}, u32[]{:S(2)}) collective-permute-start(bf16[96,128]{1,0:T(8,128)(2,1)S(1)} %get-tuple-element.59), channel_id=1, source_target_pairs={{16,8},{17,9},{18,10},{19,11},{20,12},{21,13},{22,14},{23,15},{8,0... | collective-permute-start | bytes 73736 | tf_op jit(solution)/shard_map/ppermute | solution.py:323
  19.6 4.3 %collective-permute-start.10 = (bf16[96,128]{1,0:T(8,128)(2,1)S(1)}, bf16[96,128]{1,0:T(8,128)(2,1)S(1)}, u32[]{:S(2)}, u32[]{:S(2)}) collective-permute-start(bf16[96,128]{1,0:T(8,128)(2,1)S(1)} %get-tuple-element.63), channel_id=1, source_target_pairs={{8,1},{9,0},{10,3},{11,2},{12,5},{13,4},{14,7},{15,6},{0,8},{1,9},... | collective-permute-start | bytes 73736 | tf_op jit(solution)/shard_map/ppermute | solution.py:323
  22.6 1.2 %collective-permute-start.11 = (bf16[96,128]{1,0:T(8,128)(2,1)S(1)}, bf16[96,128]{1,0:T(8,128)(2,1)S(1)}, u32[]{:S(2)}, u32[]{:S(2)}) collective-permute-start(bf16[96,128]{1,0:T(8,128)(2,1)S(1)} %get-tuple-element.64), channel_id=1, source_target_pairs={{8,0},{9,1},{10,2},{11,3},{12,4},{13,5},{14,6},{15,7},{0,8},{1,9},... | collective-permute-start | bytes 73736 | tf_op jit(solution)/shard_map/ppermute | solution.py:323
  22.7 5.9 %collective-permute-start.8 = (bf16[96,128]{1,0:T(8,128)(2,1)S(1)}, bf16[96,128]{1,0:T(8,128)(2,1)S(1)}, u32[]{:S(2)}, u32[]{:S(2)}) collective-permute-start(bf16[96,128]{1,0:T(8,128)(2,1)S(1)} %get-tuple-element.61), channel_id=1, source_target_pairs={{8,7},{9,2},{10,1},{11,4},{12,3},{13,6},{14,5},{15,0},{0,16},{1,17... | collective-permute-start | bytes 73736 | tf_op jit(solution)/shard_map/ppermute | solution.py:323
  22.7 5.9 %collective-permute-start.9 = (bf16[96,128]{1,0:T(8,128)(2,1)S(1)}, bf16[96,128]{1,0:T(8,128)(2,1)S(1)}, u32[]{:S(2)}, u32[]{:S(2)}) collective-permute-start(bf16[96,128]{1,0:T(8,128)(2,1)S(1)} %get-tuple-element.62), channel_id=1, source_target_pairs={{8,4},{9,5},{10,6},{11,7},{12,0},{13,1},{14,2},{15,3},{0,16},{1,17... | collective-permute-start | bytes 73736 | tf_op jit(solution)/shard_map/ppermute | solution.py:323
  30.3 2.3 %collective-permute-start.12 = (bf16[96,128]{1,0:T(8,128)(2,1)S(1)}, bf16[96,128]{1,0:T(8,128)(2,1)S(1)}, u32[]{:S(2)}, u32[]{:S(2)}) collective-permute-start(bf16[96,128]{1,0:T(8,128)(2,1)S(1)} %get-tuple-element.66), channel_id=1, source_target_pairs={{0,31},{1,26},{2,25},{3,28},{4,27},{5,30},{6,29},{7,24},{24,16},{2... | collective-permute-start | bytes 73736 | tf_op jit(solution)/shard_map/ppermute | solution.py:323
  30.4 2.2 %collective-permute-start.13 = (bf16[96,128]{1,0:T(8,128)(2,1)S(1)}, bf16[96,128]{1,0:T(8,128)(2,1)S(1)}, u32[]{:S(2)}, u32[]{:S(2)}) collective-permute-start(bf16[96,128]{1,0:T(8,128)(2,1)S(1)} %get-tuple-element.67), channel_id=1, source_target_pairs={{0,28},{1,29},{2,30},{3,31},{4,24},{5,25},{6,26},{7,27},{24,16},{2... | collective-permute-start | bytes 73736 | tf_op jit(solution)/shard_map/ppermute | solution.py:323
  30.5 2.2 %collective-permute-start.14 = (bf16[96,128]{1,0:T(8,128)(2,1)S(1)}, bf16[96,128]{1,0:T(8,128)(2,1)S(1)}, u32[]{:S(2)}, u32[]{:S(2)}) collective-permute-start(bf16[96,128]{1,0:T(8,128)(2,1)S(1)} %get-tuple-element.68), channel_id=1, source_target_pairs={{0,25},{1,24},{2,27},{3,26},{4,29},{5,28},{6,31},{7,30},{24,16},{2... | collective-permute-start | bytes 73736 | tf_op jit(solution)/shard_map/ppermute | solution.py:323
  30.5 3.7 %collective-permute-start.15 = (bf16[96,128]{1,0:T(8,128)(2,1)S(1)}, bf16[96,128]{1,0:T(8,128)(2,1)S(1)}, u32[]{:S(2)}, u32[]{:S(2)}) collective-permute-start(bf16[96,128]{1,0:T(8,128)(2,1)S(1)} %get-tuple-element.69), channel_id=1, source_target_pairs={{0,24},{1,25},{2,26},{3,27},{4,28},{5,29},{6,30},{7,31},{24,16},{2... | collective-permute-start | bytes 73736 | tf_op jit(solution)/shard_map/ppermute | solution.py:323
  34.3 3.8 %collective-permute-start.16 = (bf16[96,128]{1,0:T(8,128)(2,1)S(1)}, bf16[96,128]{1,0:T(8,128)(2,1)S(1)}, u32[]{:S(2)}, u32[]{:S(2)}) collective-permute-start(bf16[96,128]{1,0:T(8,128)(2,1)S(1)} %get-tuple-element.71), channel_id=1, source_target_pairs={{24,23},{25,18},{26,17},{27,20},{28,19},{29,22},{30,21},{31,16},{1... | collective-permute-start | bytes 73736 | tf_op jit(solution)/shard_map/ppermute | solution.py:323
  34.7 3.8 %collective-permute-start.17 = (bf16[96,128]{1,0:T(8,128)(2,1)S(1)}, bf16[96,128]{1,0:T(8,128)(2,1)S(1)}, u32[]{:S(2)}, u32[]{:S(2)}) collective-permute-start(bf16[96,128]{1,0:T(8,128)(2,1)S(1)} %get-tuple-element.72), channel_id=1, source_target_pairs={{24,20},{25,21},{26,22},{27,23},{28,16},{29,17},{30,18},{31,19},{1... | collective-permute-start | bytes 73736 | tf_op jit(solution)/shard_map/ppermute | solution.py:323
  37.1 1.4 %collective-permute-start.18 = (bf16[96,128]{1,0:T(8,128)(2,1)S(1)}, bf16[96,128]{1,0:T(8,128)(2,1)S(1)}, u32[]{:S(2)}, u32[]{:S(2)}) collective-permute-start(bf16[96,128]{1,0:T(8,128)(2,1)S(1)} %get-tuple-element.73), channel_id=1, source_target_pairs={{24,17},{25,16},{26,19},{27,18},{28,21},{29,20},{30,23},{31,22},{1... | collective-permute-start | bytes 73736 | tf_op jit(solution)/shard_map/ppermute | solution.py:323
  37.2 1.4 %collective-permute-start.19 = (bf16[96,128]{1,0:T(8,128)(2,1)S(1)}, bf16[96,128]{1,0:T(8,128)(2,1)S(1)}, u32[]{:S(2)}, u32[]{:S(2)}) collective-permute-start(bf16[96,128]{1,0:T(8,128)(2,1)S(1)} %get-tuple-element.74), channel_id=1, source_target_pairs={{24,16},{25,17},{26,18},{27,19},{28,20},{29,21},{30,22},{31,23},{1... | collective-permute-start | bytes 73736 | tf_op jit(solution)/shard_map/ppermute | solution.py:323
  38.5 4.5 %collective-permute-start.20 = (bf16[96,128]{1,0:T(8,128)(2,1)S(1)}, bf16[96,128]{1,0:T(8,128)(2,1)S(1)}, u32[]{:S(2)}, u32[]{:S(2)}) collective-permute-start(bf16[96,128]{1,0:T(8,128)(2,1)S(1)} %get-tuple-element.75), channel_id=1, source_target_pairs={{16,15},{17,10},{18,9},{19,12},{20,11},{21,14},{22,13},{23,8},{8,0... | collective-permute-start | bytes 73736 | tf_op jit(solution)/shard_map/ppermute | solution.py:323
  40.3 4.1 %collective-permute-start.21 = (bf16[96,128]{1,0:T(8,128)(2,1)S(1)}, bf16[96,128]{1,0:T(8,128)(2,1)S(1)}, u32[]{:S(2)}, u32[]{:S(2)}) collective-permute-start(bf16[96,128]{1,0:T(8,128)(2,1)S(1)} %get-tuple-element.76), channel_id=1, source_target_pairs={{16,12},{17,13},{18,14},{19,15},{20,8},{21,9},{22,10},{23,11},{8,0... | collective-permute-start | bytes 73736 | tf_op jit(solution)/shard_map/ppermute | solution.py:323
  42.9 1.8 %collective-permute-start.22 = (bf16[96,128]{1,0:T(8,128)(2,1)S(1)}, bf16[96,128]{1,0:T(8,128)(2,1)S(1)}, u32[]{:S(2)}, u32[]{:S(2)}) collective-permute-start(bf16[96,128]{1,0:T(8,128)(2,1)S(1)} %get-tuple-element.77), channel_id=1, source_target_pairs={{16,9},{17,8},{18,11},{19,10},{20,13},{21,12},{22,15},{23,14},{8,0... | collective-permute-start | bytes 73736 | tf_op jit(solution)/shard_map/ppermute | solution.py:323
  42.9 1.9 %collective-permute-start.23 = (bf16[96,128]{1,0:T(8,128)(2,1)S(1)}, bf16[96,128]{1,0:T(8,128)(2,1)S(1)}, u32[]{:S(2)}, u32[]{:S(2)}) collective-permute-start(bf16[96,128]{1,0:T(8,128)(2,1)S(1)} %get-tuple-element.78), channel_id=1, source_target_pairs={{16,8},{17,9},{18,10},{19,11},{20,12},{21,13},{22,14},{23,15},{8,0... | collective-permute-start | bytes 73736 | tf_op jit(solution)/shard_map/ppermute | solution.py:323
  44.9 5.9 %collective-permute-start.24 = (bf16[96,128]{1,0:T(8,128)(2,1)S(1)}, bf16[96,128]{1,0:T(8,128)(2,1)S(1)}, u32[]{:S(2)}, u32[]{:S(2)}) collective-permute-start(bf16[96,128]{1,0:T(8,128)(2,1)S(1)} %get-tuple-element.79), channel_id=1, source_target_pairs={{8,7},{9,2},{10,1},{11,4},{12,3},{13,6},{14,5},{15,0},{0,16},{1,17... | collective-permute-start | bytes 73736 | tf_op jit(solution)/shard_map/ppermute | solution.py:323
  46.5 5.2 %collective-permute-start.25 = (bf16[96,128]{1,0:T(8,128)(2,1)S(1)}, bf16[96,128]{1,0:T(8,128)(2,1)S(1)}, u32[]{:S(2)}, u32[]{:S(2)}) collective-permute-start(bf16[96,128]{1,0:T(8,128)(2,1)S(1)} %get-tuple-element.80), channel_id=1, source_target_pairs={{8,4},{9,5},{10,6},{11,7},{12,0},{13,1},{14,2},{15,3},{0,16},{1,17... | collective-permute-start | bytes 73736 | tf_op jit(solution)/shard_map/ppermute | solution.py:323
  47.1 4.7 %collective-permute-start.26 = (bf16[96,128]{1,0:T(8,128)(2,1)S(1)}, bf16[96,128]{1,0:T(8,128)(2,1)S(1)}, u32[]{:S(2)}, u32[]{:S(2)}) collective-permute-start(bf16[96,128]{1,0:T(8,128)(2,1)S(1)} %get-tuple-element.81), channel_id=1, source_target_pairs={{8,1},{9,0},{10,3},{11,2},{12,5},{13,4},{14,7},{15,6},{0,8},{1,9},... | collective-permute-start | bytes 73736 | tf_op jit(solution)/shard_map/ppermute | solution.py:323
  47.6 4.2 %collective-permute-start.27 = (bf16[96,128]{1,0:T(8,128)(2,1)S(1)}, bf16[96,128]{1,0:T(8,128)(2,1)S(1)}, u32[]{:S(2)}, u32[]{:S(2)}) collective-permute-start(bf16[96,128]{1,0:T(8,128)(2,1)S(1)} %get-tuple-element.82), channel_id=1, source_target_pairs={{8,0},{9,1},{10,2},{11,3},{12,4},{13,5},{14,6},{15,7},{0,8},{1,9},... | collective-permute-start | bytes 73736 | tf_op jit(solution)/shard_map/ppermute | solution.py:323
  53.2 3.9 %collective-permute-start.28 = (bf16[96,128]{1,0:T(8,128)(2,1)S(1)}, bf16[96,128]{1,0:T(8,128)(2,1)S(1)}, u32[]{:S(2)}, u32[]{:S(2)}) collective-permute-start(bf16[96,128]{1,0:T(8,128)(2,1)S(1)} %get-tuple-element.83), channel_id=1, source_target_pairs={{0,15},{1,10},{2,9},{3,12},{4,11},{5,14},{6,13},{7,8},{8,24},{9,25... | collective-permute-start | bytes 73736 | tf_op jit(solution)/shard_map/ppermute | solution.py:323
  53.2 4.3 %collective-permute-start.29 = (bf16[96,128]{1,0:T(8,128)(2,1)S(1)}, bf16[96,128]{1,0:T(8,128)(2,1)S(1)}, u32[]{:S(2)}, u32[]{:S(2)}) collective-permute-start(bf16[96,128]{1,0:T(8,128)(2,1)S(1)} %get-tuple-element.84), channel_id=1, source_target_pairs={{0,12},{1,13},{2,14},{3,15},{4,8},{5,9},{6,10},{7,11},{8,24},{9,25... | collective-permute-start | bytes 73736 | tf_op jit(solution)/shard_map/ppermute | solution.py:323
  53.3 4.2 %collective-permute-start.30 = (bf16[96,128]{1,0:T(8,128)(2,1)S(1)}, bf16[96,128]{1,0:T(8,128)(2,1)S(1)}, u32[]{:S(2)}, u32[]{:S(2)}) collective-permute-start(bf16[96,128]{1,0:T(8,128)(2,1)S(1)} %get-tuple-element.85), channel_id=1, source_target_pairs={{0,9},{1,8},{2,11},{3,10},{4,13},{5,12},{6,15},{7,14},{8,0},{9,1},... | collective-permute-start | bytes 73736 | tf_op jit(solution)/shard_map/ppermute | solution.py:323
  53.4 4.1 %collective-permute-start.31 = (bf16[96,128]{1,0:T(8,128)(2,1)S(1)}, bf16[96,128]{1,0:T(8,128)(2,1)S(1)}, u32[]{:S(2)}, u32[]{:S(2)}) collective-permute-start(bf16[96,128]{1,0:T(8,128)(2,1)S(1)} %get-tuple-element.86), channel_id=1, source_target_pairs={{0,8},{1,9},{2,10},{3,11},{4,12},{5,13},{6,14},{7,15},{8,0},{9,1},... | collective-permute-start | bytes 73736 | tf_op jit(solution)/shard_map/ppermute | solution.py:323
  53.9 4.0 %collective-permute-start.33 = (f32[1,6,16,128]{3,2,1,0:T(8,128)S(1)}, f32[1,6,16,128]{3,2,1,0:T(8,128)S(1)}, u32[]{:S(2)}, u32[]{:S(2)}) collective-permute-start(f32[1,6,16,128]{3,2,1,0:T(8,128)S(1)} %shard_map.73), channel_id=1, source_target_pairs={{0,8},{8,16},{16,24},{24,0},{1,9},{9,17},{17,25},{25,1},{2,10},{10... | collective-permute-start | bytes 147464 | tf_op jit(solution)/shard_map/ppermute | solution.py:328
  57.5 1.3 %collective-permute-start.32 = (f32[1,6,16,128]{3,2,1,0:T(8,128)S(1)}, f32[1,6,16,128]{3,2,1,0:T(8,128)S(1)}, u32[]{:S(2)}, u32[]{:S(2)}) collective-permute-start(f32[1,6,16,128]{3,2,1,0:T(8,128)S(1)} %shard_map.72), channel_id=1, source_target_pairs={{0,8},{8,0},{16,24},{24,16},{1,9},{9,1},{17,25},{25,17},{2,10},{10... | collective-permute-start | bytes 147464 | tf_op jit(solution)/shard_map/ppermute | solution.py:330
